TPU v7x, 128 devices: a whole 4x4x4 slice. The times are simulated.
128 devices in a mesh: row: 16 (over z_hi, y, core), col: 8 (over z_lo, x).
Axes of the slice: x: 4, y: 4, z: 4 (z_hi: 2, z_lo: 2; z = z_hi * 2 + z_lo), core: 2. Of those that a mesh axis runs over, the one named last changes fastest.
Arguments:
- token_ids: int32 [16384], P(('row', 'col')), may hold values from 0 to 511
- embedding: bfloat16 [512, 8192], replicated, may hold values from -6 to 6
- norm_gain: bfloat16 [8192], replicated, may hold values from 0.099609375 to 1.8984375
- w_in: bfloat16 [8192, 12288], P(None, ('row', 'col')), may hold values from -0.0625 to 0.0625
- short_taps: float32 [7, 12288], replicated, may hold values from -2 to 2
- long_filter: float32 [16384, 4096], P(('row', 'col')), may hold values from -0.046875 to 0.046875
- skip_gain: float32 [4096], replicated, may hold values from -1 to 1
Outputs:
- mixed_out: bfloat16 [16384, 4096], P(('row', 'col'))
All inputs are finite; a program needn't handle non-finite values.
Results may differ from a plain program's by a relative error of at most 0.0095.
Values may be sent and summed in bfloat16 or wider, within the bound.
No kernel may reach another device: no remote copies, remote signals or barrier semaphores. Data moves between devices by JAX's collectives and lax.ppermute only.
A program may use at most 192 MiB of HBM per device.

v0:
```python
import math

import jax
import jax.numpy as jnp
from jax import lax
from jax.sharding import PartitionSpec as P

FFT_COLS = 128


EPSILON = 1e-05


def passed_along(x, axis, by):
    length = lax.axis_size(axis)
    pairs = [(i, i + by) for i in range(length) if 0 <= i + by < length]
    return lax.ppermute(x, axis, pairs)


def phase_table(first_index, second_index, period):
    turns = first_index * second_index % period
    return 2.0 * math.pi / period * turns.astype(jnp.float32)


def contract(form, table_part, data_part):
    return jnp.einsum(form, table_part, data_part, precision=lax.Precision.HIGHEST)


def project_table(embedding, norm_gain, w_in):
    rows_f32 = embedding.astype(jnp.float32)
    inverse_rms = lax.rsqrt(jnp.mean(rows_f32 * rows_f32, axis=1, keepdims=True) + EPSILON)
    normed = (rows_f32 * inverse_rms * norm_gain.astype(jnp.float32)).astype(jnp.bfloat16)
    own_columns = jnp.dot(normed, w_in, preferred_element_type=jnp.float32).astype(jnp.bfloat16)
    return lax.all_gather(own_columns, ("row", "col"), axis=1, tiled=True)


def short_filter(mixed_rows, short_taps):
    tap_count = short_taps.shape[0]
    row_count = mixed_rows.shape[0]
    earlier = passed_along(mixed_rows[row_count - (tap_count - 1) :], ("row", "col"), 1)
    extended = jnp.concatenate([earlier, mixed_rows], axis=0).astype(jnp.float32)
    result = short_taps[0] * extended[tap_count - 1 :]
    for offset in range(1, tap_count):
        begin_at = tap_count - 1 - offset
        result = result + short_taps[offset] * extended[begin_at : begin_at + row_count]
    return result


def local_causal(signal_all, filter_all):
    seq_len = signal_all.shape[0]
    width = signal_all.shape[1]
    short_len = seq_len // FFT_COLS
    first_len = 2 * short_len
    total_len = first_len * FFT_COLS
    angle_one = phase_table(
        lax.iota(jnp.int32, short_len)[:, None], lax.iota(jnp.int32, first_len)[None, :], first_len
    )
    cos_one = jnp.cos(angle_one)
    sin_one = jnp.sin(angle_one)
    angle_twist = phase_table(
        lax.iota(jnp.int32, first_len)[:, None], lax.iota(jnp.int32, FFT_COLS)[None, :], total_len
    )
    cos_twist = jnp.cos(angle_twist)
    sin_twist = jnp.sin(angle_twist)
    angle_two = phase_table(
        lax.iota(jnp.int32, FFT_COLS)[:, None], lax.iota(jnp.int32, FFT_COLS)[None, :], FFT_COLS
    )
    cos_two = jnp.cos(angle_two)
    sin_two = jnp.sin(angle_two)

    def forward(series):
        blocked = series.reshape(short_len, FFT_COLS, width)
        real_part = contract("sk,sjc->ckj", cos_one, blocked)
        imag_part = -contract("sk,sjc->ckj", sin_one, blocked)
        turned_re = real_part * cos_twist + imag_part * sin_twist
        turned_im = imag_part * cos_twist - real_part * sin_twist
        out_re = contract("jm,ckj->ckm", cos_two, turned_re) + contract(
            "jm,ckj->ckm", sin_two, turned_im
        )
        out_im = contract("jm,ckj->ckm", cos_two, turned_im) - contract(
            "jm,ckj->ckm", sin_two, turned_re
        )
        return (out_re, out_im)

    signal_re, signal_im = forward(signal_all)
    filter_re, filter_im = forward(filter_all)
    product_re = signal_re * filter_re - signal_im * filter_im
    product_im = signal_re * filter_im + signal_im * filter_re
    back_re = contract("jm,ckm->ckj", cos_two, product_re) - contract(
        "jm,ckm->ckj", sin_two, product_im
    )
    back_im = contract("jm,ckm->ckj", cos_two, product_im) + contract(
        "jm,ckm->ckj", sin_two, product_re
    )
    turned_re = back_re * cos_twist - back_im * sin_twist
    turned_im = back_im * cos_twist + back_re * sin_twist
    summed = contract("sk,ckj->sjc", cos_one, turned_re) - contract(
        "sk,ckj->sjc", sin_one, turned_im
    )
    return (summed * (1.0 / total_len)).reshape(seq_len, width)


def local(token_ids, embedding, norm_gain, w_in, short_taps, long_filter, skip_gain):
    lookup_table = project_table(embedding, norm_gain, w_in)
    vocab_size = lookup_table.shape[0]
    one_hot = (token_ids[:, None] == lax.iota(jnp.int32, vocab_size)[None, :]).astype(jnp.bfloat16)
    mixed_rows = jnp.dot(one_hot, lookup_table, preferred_element_type=jnp.float32).astype(
        jnp.bfloat16
    )
    filtered = short_filter(mixed_rows, short_taps)
    channels = filtered.shape[1] // 3
    gate_out = filtered[:, :channels]
    signal = filtered[:, channels : 2 * channels] * filtered[:, 2 * channels :]
    signal_all, filter_all = (
        lax.all_to_all(signal, ("row", "col"), split_axis=1, concat_axis=0, tiled=True),
        lax.all_to_all(long_filter, ("row", "col"), split_axis=1, concat_axis=0, tiled=True),
    )
    causal_all = local_causal(signal_all, filter_all)
    long_part = lax.all_to_all(causal_all, ("row", "col"), split_axis=0, concat_axis=1, tiled=True)
    mixed_out = gate_out * (long_part + skip_gain * signal)
    return mixed_out.astype(jnp.bfloat16)


def solution(mesh):
    in_specs = (
        P(("row", "col")),
        P(),
        P(),
        P(None, ("row", "col")),
        P(),
        P(("row", "col"), None),
        P(),
    )
    out_specs = P(("row", "col"), None)
    return jax.shard_map(local, mesh=mesh, in_specs=in_specs, out_specs=out_specs, check_vma=False)
```

profile of v0, /device:TPU:0, one launch (start us, length us, event | category | flops | bytes accessed | tf_op | source)
XLA Modules:
  0.0 561.6 jit_solution(3965734877258306150)
XLA Ops:
  6.5 0.0 copy-start
  6.5 0.0 copy-start.9
  6.5 0.0 all-gather.2.cloned.1.call-start
  6.5 0.0 copy-start.6
  6.5 5.3 fusion
  11.8 0.0 copy-done.9
  11.8 0.0 copy-done
  11.8 1.0 copy-done.6
  12.8 3.7 fusion.54
  16.5 0.0 all-gather.2.cloned.1.call-update
  16.5 0.0 copy-start.7
  16.5 3.0 copy.44
  19.5 11.7 %all-to-all-start.1 = ((f32[128,128,32]{0,2,1:T(8,128)}), f32[128,128,32]{0,2,1:T(8,128)}, u32[]{:S(2)}, u32[]{:S(2)}) async-start(f32[128,128,32]{0,2,1:T(8,128)} %bitcast.114), calls=%async_computation.1 | async-start | bytes 4194304 | tf_op jit(solution)/shard_map/all_to_all | solution.py:116
  31.2 0.0 copy-start.10
  31.2 0.5 fusion.101
  31.7 0.1 copy.49
  31.8 0.1 copy.47
  31.9 0.0 copy-done.7
  31.9 0.2 fusion.198
  32.2 30.5 %all-to-all-done.1 = f32[128,128,32]{0,2,1:T(8,128)} async-done(((f32[128,128,32]{0,2,1:T(8,128)}), f32[128,128,32]{0,2,1:T(8,128)}, u32[]{:S(2)}, u32[]{:S(2)}) %all-to-all-start.1) | async-done | bytes 2097184 | tf_op jit(solution)/shard_map/all_to_all | solution.py:116
  62.7 9.3 %fusion.38 = f32[256,128,32]{1,0,2:T(8,128)} fusion(f32[128,128,32]{0,2,1:T(8,128)} %all-to-all-done.1), kind=kOutput, calls=%fused_computation.58 | convolution fusion | flops 1611071488 | bytes 6291456 | tf_op jit(solution)/shard_map/sk,sjc->ckj/dot_general | solution.py:26
  71.9 281.6 %all-gather.2.cloned.1.call-done = bf16[512,12288]{0,1:T(8,128)(2,1)} async-done(((bf16[512,96]{0,1:T(8,128)(2,1)}), bf16[512,12288]{0,1:T(8,128)(2,1)}) %all-gather.2.cloned.1.call-update) | async-done | bytes 12582928 | tf_op jit(solution)/shard_map/all_gather | solution.py:34
  353.6 0.0 copy-done.10
  353.6 8.8 %convolution_convert_fusion = bf16[128,12288]{1,0:T(8,128)(2,1)S(1)} fusion(bf16[512,12288]{0,1:T(8,128)(2,1)} %all-gather.2.cloned.1.call-done, s32[128]{0:T(128)S(1)} %copy-done.10), kind=kOutput, calls=%fused_computation.5 | convolution fusion | flops 1612251136 | bytes 15729152 | tf_op jit(solution)/shard_map/dot_general | solution.py:107
  362.4 3.9 collective-permute-start
  366.3 9.3 %fusion.40 = f32[256,128,32]{1,0,2:T(8,128)} fusion(f32[128,128,32]{0,2,1:T(8,128)} %all-to-all-done.1), kind=kOutput, calls=%fused_computation.60 | convolution fusion | flops 1611071488 | bytes 6291456 | tf_op jit(solution)/shard_map/sk,sjc->ckj/dot_general | solution.py:26
  375.6 0.0 collective-permute-done
  375.6 0.9 maximum_convert_fusion
  376.5 5.2 fusion.7
  381.7 0.0 copy-start.4
  381.7 2.7 copy-done.4
  384.3 1.6 slice_multiply_fusion.7
  385.9 2.9 copy.40
  388.8 11.1 %all-to-all-start = ((f32[128,128,32]{0,2,1:T(8,128)}), f32[128,128,32]{0,2,1:T(8,128)}, u32[]{:S(2)}, u32[]{:S(2)}) async-start(f32[128,128,32]{0,2,1:T(8,128)} %bitcast.115), calls=%async_computation | async-start | bytes 4194304 | tf_op jit(solution)/shard_map/all_to_all | solution.py:115
  399.9 0.0 copy-start.2
  399.9 0.0 copy-start.3
  399.9 6.8 %fusion.13 = f32[32,256,128]{2,1,0:T(8,128)S(1)} fusion(f32[256,128,32]{1,0,2:T(8,128)} %fusion.40, f32[256,128,32]{1,0,2:T(8,128)} %fusion.38, f32[256,128]{1,0:T(8,128)S(1)} %copy.49, f32[256,128]{1,0:T(8,128)S(1)} %copy.47), kind=kOutput, calls=%fused_computation.22 | convolution fusion | flops 1615036416 | bytes 12845056 | tf_op jit(solution)/shard_map/jm,ckj->ckm/dot_general | solution.py:26
  406.7 0.0 copy-done.2
  406.7 0.0 copy-done.3
  406.7 4.2 fusion.15
  410.9 5.8 %fusion.34 = f32[32,256,128]{2,1,0:T(8,128)} fusion(f32[32,256,128]{2,1,0:T(8,128)S(1)} %fusion.13, f32[256,128,32]{1,0,2:T(8,128)S(1)} %copy-done.3, f32[256,128,32]{1,0,2:T(8,128)S(1)} %copy-done.2, f32[256,128]{1,0:T(8,128)S(1)} %copy.49, f32[256,128]{1,0:T(8,128)S(1)} %copy.47), kind=kOutput, calls=%fused_computation.50 | convolution fusion | flops 1616084992 | bytes 17039360 | tf_op jit(solution)/shard_map/jm,ckj->ckm/dot_general | solution.py:26
  416.7 5.8 %fusion.31 = f32[32,256,128]{2,1,0:T(8,128)} fusion(f32[32,256,128]{2,1,0:T(8,128)S(1)} %fusion.15, f32[256,128,32]{1,0,2:T(8,128)S(1)} %copy-done.3, f32[256,128,32]{1,0,2:T(8,128)S(1)} %copy-done.2, f32[256,128]{1,0:T(8,128)S(1)} %copy.49, f32[256,128]{1,0:T(8,128)S(1)} %copy.47), kind=kOutput, calls=%fused_computation.49 | convolution fusion | flops 1616084992 | bytes 17039360 | tf_op jit(solution)/shard_map/jm,ckj->ckm/dot_general | solution.py:26
  422.5 6.8 %all-to-all-done = f32[128,128,32]{0,2,1:T(8,128)} async-done(((f32[128,128,32]{0,2,1:T(8,128)}), f32[128,128,32]{0,2,1:T(8,128)}, u32[]{:S(2)}, u32[]{:S(2)}) %all-to-all-start) | async-done | bytes 2097184 | tf_op jit(solution)/shard_map/all_to_all | solution.py:115
  429.3 3.1 copy.41
  432.4 0.0 copy-start.5
  432.5 5.7 %fusion.42 = f32[128,32,256]{2,0,1:T(8,128)S(1)} fusion(f32[128,128,32]{1,0,2:T(8,128)} %copy.41), kind=kOutput, calls=%fused_computation.62 | convolution fusion | flops 1611071488 | bytes 6291456 | tf_op jit(solution)/shard_map/sk,sjc->ckj/dot_general | solution.py:26
  438.2 0.0 copy-done.5
  438.2 4.0 fusion.44
  442.2 9.4 %fusion.57 = f32[32,256,128]{2,1,0:T(8,128)} fusion(f32[128,32,256]{2,0,1:T(8,128)S(1)} %fusion.44, f32[128,32,256]{2,0,1:T(8,128)S(1)} %fusion.42, f32[256,128]{0,1:T(8,128)S(1)} %get-tuple-element.14, f32[256,128]{0,1:T(8,128)S(1)} %get-tuple-element.15), kind=kOutput, calls=%fused_computation.74 | convolution fusion | flops 1615036416 | bytes 12845056 | tf_op jit(solution)/shard_map/jm,ckj->ckm/dot_general | solution.py:26
  451.6 7.4 %fusion.61 = f32[32,256,128]{2,1,0:T(8,128)S(1)} fusion(f32[128,32,256]{2,0,1:T(8,128)S(1)} %fusion.44, f32[128,32,256]{2,0,1:T(8,128)S(1)} %fusion.42, f32[256,128]{0,1:T(8,128)S(1)} %get-tuple-element.14, f32[256,128]{0,1:T(8,128)S(1)} %get-tuple-element.15), kind=kOutput, calls=%fused_computation.75 | convolution fusion | flops 1615036416 | bytes 12845056 | tf_op jit(solution)/shard_map/jm,ckj->ckm/dot_general | solution.py:26
  459.0 9.1 %convolution_add_fusion.1 = f32[32,256,128]{2,1,0:T(8,128)} fusion(f32[32,256,128]{2,1,0:T(8,128)S(1)} %fusion.61, f32[128,32,256]{2,0,1:T(8,128)S(1)} %fusion.44, f32[128,32,256]{2,0,1:T(8,128)S(1)} %fusion.42, f32[256,128]{0,1:T(8,128)S(1)} %get-tuple-element.14, f32[256,128]{0,1:T(8,128)S(1)} %get-tuple-element.15), kind=kOutput, calls=%fused_computation.54 | convolution fusion | flops 1616084992 | bytes 17039360 | tf_op jit(solution)/shard_map/jm,ckj->ckm/dot_general | solution.py:26
  468.1 11.9 %multiply_add_fusion = (f32[32,256,128]{2,1,0:T(8,128)S(1)}, f32[32,256,128]{2,1,0:T(8,128)S(1)}) fusion(f32[32,256,128]{2,1,0:T(8,128)} %fusion.31, f32[32,256,128]{2,1,0:T(8,128)} %convolution_add_fusion.1, f32[32,256,128]{2,1,0:T(8,128)} %fusion.34, f32[32,256,128]{2,1,0:T(8,128)} %fusion.57, f32[128,32,256]{2,0,1:T(8,128)S(1)} %fusion.44, ...), kind=kOutput, calls=%fused_computation.44 | convolution fusion | flops 1622376448 | bytes 33816576 | tf_op jit(solution)/shard_map/jm,ckj->ckm/dot_general | solution.py:26
  480.1 4.2 fusion.91
  484.2 4.2 fusion.93
  488.4 4.9 convolution_add_fusion
  493.3 4.2 convolution_subtract_fusion
  497.6 4.2 fusion.23
  501.7 5.8 %multiply_bitcast_fusion = f32[128,128,32]{0,1,2:T(8,128)} fusion(f32[32,128,128]{2,1,0:T(8,128)S(1)} %fusion.23, f32[32,256,128]{1,2,0:T(8,128)S(1)} %convolution_add_fusion, f32[32,256,128]{1,2,0:T(8,128)S(1)} %convolution_subtract_fusion, f32[256,128]{0,1:T(8,128)S(1)} %get-tuple-element.14, f32[256,128]{0,1:T(8,128)S(1)} %get-tuple-element.15), kind=kOutput, calls=%fused_computation.66 | convolution fusion | flops 1615265792 | bytes 12845056 | tf_op jit(solution)/shard_map/sk,ckj->sjc/dot_general | solution.py:26
  507.5 3.1 copy.56
  510.7 35.6 %all_to_all.48 = f32[128,128,32]{1,2,0:T(8,128)} all-to-all(f32[128,128,32]{1,2,0:T(8,128)} %copy.56), channel_id=1, replica_groups=mesh['row'=16,'col'=8] {'row','col'}, dimensions={0} | all-to-all | bytes 4194304 | tf_op jit(solution)/shard_map/all_to_all | solution.py:119
  546.2 3.0 copy.57
  549.2 0.0 copy-done.8
  549.2 5.0 fusion.37
  554.3 0.0 copy-done.1
  (5 shorter events, 0.1 us)
Async XLA Ops:
  6.5 5.3 copy-start
  6.5 5.3 copy-start.9
  6.5 347.0 %all-gather.2.cloned.1.call-start = ((), (), s32[]{:S(2)}) async-start(), calls=%async_computation.3 | async-start | bytes 12681216 | tf_op jit(solution)/shard_map/all_gather | solution.py:34
  6.5 6.3 %copy-start.6 = (bf16[512,8192]{1,0:T(8,128)(2,1)S(1)}, bf16[512,8192]{1,0:T(8,128)(2,1)}, u32[]{:S(2)}) copy-start(bf16[512,8192]{1,0:T(8,128)(2,1)} %param.8) | copy-start | bytes 25165828
  16.5 15.4 %copy-start.7 = (f32[7,12288]{1,0:T(8,128)S(1)}, f32[7,12288]{1,0:T(8,128)}, u32[]{:S(2)}) copy-start(f32[7,12288]{1,0:T(8,128)} %param.11) | copy-start | bytes 1032196
  19.5 43.2 %all-to-all-start.1 = ((f32[128,128,32]{0,2,1:T(8,128)}), f32[128,128,32]{0,2,1:T(8,128)}, u32[]{:S(2)}, u32[]{:S(2)}) async-start(f32[128,128,32]{0,2,1:T(8,128)} %bitcast.114), calls=%async_computation.1 | async-start | bytes 4194304 | tf_op jit(solution)/shard_map/all_to_all | solution.py:116
  31.2 322.4 %copy-start.10 = (s32[128]{0:T(128)S(1)}, s32[128]{0:T(128)}, u32[]{:S(2)}) copy-start(s32[128]{0:T(128)} %param.7) | copy-start | bytes 1540
  362.4 13.2 %collective-permute-start = (bf16[6,12288]{1,0:T(8,128)(2,1)S(1)}, bf16[6,12288]{1,0:T(8,128)(2,1)S(1)}, u32[]{:S(2)}, u32[]{:S(2)}) collective-permute-start(bf16[6,12288]{1,0:T(8,128)(2,1)S(1)} %slice.72), channel_id=1, source_target_pairs={{0,1},{1,2},{2,3},{3,4},{4,5},{5,6},{6,7},{7,8},{8,9},{9,10},{10,1... | collective-permute-start | bytes 442376 | tf_op jit(solution)/shard_map/ppermute | solution.py:17
  381.7 2.7 copy-start.4
  388.8 40.5 %all-to-all-start = ((f32[128,128,32]{0,2,1:T(8,128)}), f32[128,128,32]{0,2,1:T(8,128)}, u32[]{:S(2)}, u32[]{:S(2)}) async-start(f32[128,128,32]{0,2,1:T(8,128)} %bitcast.115), calls=%async_computation | async-start | bytes 4194304 | tf_op jit(solution)/shard_map/all_to_all | solution.py:115
  399.9 6.8 %copy-start.2 = (f32[256,128,32]{1,0,2:T(8,128)S(1)}, f32[256,128,32]{1,0,2:T(8,128)}, u32[]{:S(2)}) copy-start(f32[256,128,32]{1,0,2:T(8,128)} %fusion.38) | copy-start | bytes 12582916
  399.9 6.8 %copy-start.3 = (f32[256,128,32]{1,0,2:T(8,128)S(1)}, f32[256,128,32]{1,0,2:T(8,128)}, u32[]{:S(2)}) copy-start(f32[256,128,32]{1,0,2:T(8,128)} %fusion.40) | copy-start | bytes 12582916
  432.4 5.7 %copy-start.5 = (f32[128,128,32]{1,0,2:T(8,128)S(1)}, f32[128,128,32]{1,0,2:T(8,128)}, u32[]{:S(2)}) copy-start(f32[128,128,32]{1,0,2:T(8,128)} %copy.41) | copy-start | bytes 6291460
  510.7 38.6 %copy-start.8 = (f32[4096]{0:T(1024)S(1)}, f32[4096]{0:T(1024)}, u32[]{:S(2)}) copy-start(f32[4096]{0:T(1024)} %param.13) | copy-start | bytes 49156
  546.2 8.1 %copy-start.1 = (bf16[8192,96]{0,1:T(8,128)(2,1)S(1)}, bf16[8192,96]{0,1:T(8,128)(2,1)}, u32[]{:S(2)}) copy-start(bf16[8192,96]{0,1:T(8,128)(2,1)} %param.10) | copy-start | bytes 4718596
Sparse Core Ops, SparseCore 0:
  16.6 336.8 all-gather.1
where the time goes:
time: 571 us; the launch traced here: 562 us
  waiting for transfers between devices  319 us (56%)
  matrix products  129 us (23%)
  blocking collectives  35.6 us (6%)
  starting transfers between devices  26.6 us (5%)
  local copies, waits for them, and re-layouts  19.3 us (3%)
  other arithmetic  18.4 us (3%)
  between operations  14.1 us (2%)
    all_gather x1, waiting for transfers between devices, project_table(): return lax.all_gather(own_columns, ('row', 'col'), axis=1, tiled=True)  282 us
    dot_general x18, matrix products, contract(): jnp.einsum(form, table_part, data_part, precision=lax.Precision.HIGHEST)  116 us
    all_to_all x1, blocking collectives, local(): lax.all_to_all(causal_all, ('row', 'col'), split_axis=0, concat_axis=1, t...  35.6 us
    all_to_all x1, waiting for transfers between devices, local(): lax.all_to_all(long_filter, ('row', 'col'), split_axis=1, concat_axis=0,...  30.5 us
    all_to_all x1, starting transfers between devices, local(): lax.all_to_all(long_filter, ('row', 'col'), split_axis=1, concat_axis=0,...  11.7 us
  transfers between devices with their start and end apart: 4, of which 3 were waited for; matrix products, arithmetic and copies ran while one was open for 8% of the time, Pallas kernels for 0%

commit v1 on v0

v1 whole, which is shorter than its diff:
```python
import math

import jax
import jax.numpy as jnp
import numpy as np
from jax import lax
from jax.experimental import pallas as pl
from jax.experimental.pallas import tpu as pltpu
from jax.sharding import PartitionSpec as P

AXES = ("row", "col")
EPSILON = 1e-05
LANES = 128


def transform_tables(blocks, lanes):
    n = blocks * lanes
    k = np.arange(blocks)
    angle_one = 2.0 * np.pi * np.outer(4 * k + 1, np.arange(blocks)) / (4 * blocks)
    angle_twist = 2.0 * np.pi * np.outer(4 * k + 1, np.arange(lanes)) / (4 * n)
    angle_two = 2.0 * np.pi * np.outer(np.arange(lanes), np.arange(lanes)) / lanes
    first = np.concatenate([np.cos(angle_one), -np.sin(angle_one)], axis=0)
    c, s = np.cos(angle_two), np.sin(angle_two)
    second = np.block([[c, -s], [s, c]])
    second_back = np.block([[c, s], [-s, c]])
    first_back = first.T / n
    half = [x.astype(np.float32).astype(jnp.bfloat16) for x in (first, second, second_back, first_back)]
    twist = np.stack([np.cos(angle_twist), np.sin(angle_twist)]).astype(np.float32)
    return half, twist


def project_table(embedding, norm_gain, w_in):
    rows_f32 = embedding.astype(jnp.float32)
    inverse_rms = lax.rsqrt(jnp.mean(rows_f32 * rows_f32, axis=1, keepdims=True) + EPSILON)
    normed = (rows_f32 * inverse_rms * norm_gain.astype(jnp.float32)).astype(jnp.bfloat16)
    return lax.dot_general(
        w_in, normed, (((0,), (1,)), ((), ())), preferred_element_type=jnp.float32
    ).astype(jnp.bfloat16)


def forward_pair(pair, first_ref, cos, sin, second_ref):
    blocks, lanes = cos.shape
    a = jnp.dot(first_ref[...], pair, preferred_element_type=jnp.float32)
    rows = []
    for h in range(2):
        re = a[:blocks, h * lanes : (h + 1) * lanes]
        im = a[blocks:, h * lanes : (h + 1) * lanes]
        rows.append(
            jnp.concatenate([re * cos + im * sin, im * cos - re * sin], axis=1).astype(jnp.bfloat16)
        )
    turned = jnp.concatenate(rows, axis=0)
    return jnp.dot(turned, second_ref[...], preferred_element_type=jnp.float32)


def signal_kernel(
    token_ref, table_ref, taps_ref, first_ref, twist_ref, second_ref,
    gate_ref, signal_ref, spectrum_ref, taps_wide, previous,
):
    vocab = table_ref.shape[1]
    blocks, lanes = token_ref.shape
    rows = table_ref.shape[0]
    width = rows // 3
    tap_count = taps_ref.shape[1]
    for i in range(tap_count):
        taps_wide[i] = jnp.broadcast_to(taps_ref[:, i : i + 1], (rows, lanes))
    previous[...] = jnp.zeros_like(previous)
    lane = lax.broadcasted_iota(jnp.int32, (rows, lanes), 1)

    @pl.loop(0, blocks // 2)
    def _(step):
        ids = token_ref[pl.ds(2 * step, 2), :]
        entry = lax.broadcasted_iota(jnp.int32, (vocab, lanes), 0)
        one_hot = jnp.concatenate(
            [(entry == ids[h : h + 1, :]).astype(jnp.float32).astype(jnp.bfloat16) for h in range(2)], axis=1
        )
        mixed = jnp.dot(table_ref[...], one_hot, preferred_element_type=jnp.float32)
        before = previous[...]
        for h in range(2):
            here = mixed[:, h * lanes : (h + 1) * lanes]
            total = taps_wide[0] * here
            for i in range(1, tap_count):
                joined = jnp.where(lane >= lanes - i, before, here)
                total = total + taps_wide[i] * pltpu.roll(joined, i, 1)
            begin = pl.multiple_of((2 * step + h) * width, width)
            gate_ref[pl.ds(begin, width), :] = total[:width]
            signal_ref[pl.ds(begin, width), :] = total[width : 2 * width] * total[2 * width :]
            before = here
        previous[...] = before

    cos = twist_ref[0]
    sin = twist_ref[1]

    for q in range(width // 2):
        pair = jnp.concatenate(
            [signal_ref[pl.ds(2 * q + h, blocks, stride=width), :] for h in range(2)], axis=1
        ).astype(jnp.bfloat16)
        z = forward_pair(pair, first_ref, cos, sin, second_ref)
        spectrum_ref[pl.ds(2 * q * blocks, 2 * blocks), :] = z.astype(jnp.bfloat16)


def long_kernel(
    filter_ref, spectrum_ref, gate_ref, signal_ref, skip_ref, first_ref, twist_ref, second_ref,
    second_back_ref, first_back_ref, out_ref, filter_f32, long_part,
):
    blocks, lanes = twist_ref.shape[1:]
    width = skip_ref.shape[0]
    filter_f32[...] = filter_ref[...].astype(jnp.float32)
    cos = twist_ref[0]
    sin = twist_ref[1]

    for q in range(width // 2):
        pair = jnp.concatenate(
            [filter_f32[pl.ds(2 * q + h, blocks, stride=width), :] for h in range(2)], axis=1
        ).astype(jnp.bfloat16)
        f = forward_pair(pair, first_ref, cos, sin, second_ref)
        s = spectrum_ref[pl.ds(2 * q * blocks, 2 * blocks), :].astype(jnp.float32)
        f_re, f_im, s_re, s_im = f[:, :lanes], f[:, lanes:], s[:, :lanes], s[:, lanes:]
        product = jnp.concatenate(
            [f_re * s_re - f_im * s_im, f_re * s_im + f_im * s_re], axis=1
        ).astype(jnp.bfloat16)
        back = jnp.dot(product, second_back_ref[...], preferred_element_type=jnp.float32)
        columns = []
        for h in range(2):
            re = back[h * blocks : (h + 1) * blocks, :lanes]
            im = back[h * blocks : (h + 1) * blocks, lanes:]
            columns.append(jnp.concatenate([re * cos - im * sin, im * cos + re * sin], axis=0).astype(jnp.bfloat16))
        y = jnp.dot(
            first_back_ref[...], jnp.concatenate(columns, axis=1), preferred_element_type=jnp.float32
        )
        for h in range(2):
            long_part[pl.ds(2 * q + h, blocks, stride=width), :] = y[:, h * lanes : (h + 1) * lanes]

    skip = jnp.broadcast_to(skip_ref[...], (width, lanes))

    @pl.loop(0, blocks)
    def _(b):
        at = pl.ds(pl.multiple_of(b * width, width), width)
        out_ref[at, :] = (gate_ref[at, :] * (long_part[at, :] + skip * signal_ref[at, :])).astype(jnp.bfloat16)


def local(token_ids, embedding, norm_gain, w_in, short_taps, long_filter, skip_gain):
    devices = lax.axis_size(AXES)
    me = lax.axis_index(AXES)
    positions, channels = long_filter.shape
    width = channels // devices
    vocab = embedding.shape[0]
    tap_count = short_taps.shape[0]
    blocks = devices * positions // LANES
    (first, second, second_back, first_back), twist = transform_tables(blocks, LANES)

    sent_filter = long_filter.astype(jnp.bfloat16).T.reshape(devices, width, positions)
    filter_all = lax.all_to_all(sent_filter, AXES, split_axis=0, concat_axis=0, tiled=True)
    tokens_all = lax.all_to_all(
        jnp.broadcast_to(token_ids[None], (devices, positions)), AXES, split_axis=0, concat_axis=0, tiled=True
    )

    own = project_table(embedding, norm_gain, w_in)
    chunks = jnp.stack(
        [
            lax.ppermute(own[j * width : (j + 1) * width], AXES, [(d, (3 * d + j) % devices) for d in range(devices)])
            for j in range(3)
        ]
    )
    table = jnp.concatenate(
        [lax.dynamic_index_in_dim(chunks, (me + g * devices) % 3, 0, keepdims=False) for g in range(3)], axis=0
    )
    taps = lax.dynamic_index_in_dim(short_taps.reshape(tap_count, 3, devices, width), me, 2, keepdims=False)
    taps = taps.reshape(tap_count, 3 * width).T
    skip = lax.dynamic_slice_in_dim(skip_gain, me * width, width, 0)[:, None]

    rows = blocks * width
    gate, signal, spectrum = pl.pallas_call(
        signal_kernel,
        out_shape=(
            jax.ShapeDtypeStruct((rows, LANES), jnp.float32),
            jax.ShapeDtypeStruct((rows, LANES), jnp.float32),
            jax.ShapeDtypeStruct((width * blocks, 2 * LANES), jnp.bfloat16),
        ),
        scratch_shapes=[
            pltpu.VMEM((tap_count, 3 * width, LANES), jnp.float32),
            pltpu.VMEM((3 * width, LANES), jnp.float32),
        ],
        compiler_params=pltpu.CompilerParams(vmem_limit_bytes=32 * 1024 * 1024),
        name="signal_spectrum",
    )(tokens_all.reshape(blocks, LANES), table, taps, first, twist, second)
    out = pl.pallas_call(
        long_kernel,
        out_shape=jax.ShapeDtypeStruct((rows, LANES), jnp.bfloat16),
        scratch_shapes=[
            pltpu.VMEM((rows, LANES), jnp.float32),
            pltpu.VMEM((rows, LANES), jnp.float32),
        ],
        compiler_params=pltpu.CompilerParams(vmem_limit_bytes=32 * 1024 * 1024),
        name="long_convolution",
    )(filter_all.reshape(rows, LANES), spectrum, gate, signal, skip, first, twist, second, second_back, first_back)

    sent_out = out.reshape(devices, width, positions)
    received = lax.all_to_all(sent_out, AXES, split_axis=0, concat_axis=0, tiled=True)
    return received.reshape(channels, positions).T


def solution(mesh):
    in_specs = (
        P(AXES),
        P(),
        P(),
        P(None, AXES),
        P(),
        P(AXES, None),
        P(),
    )
    out_specs = P(AXES, None)
    return jax.shard_map(local, mesh=mesh, in_specs=in_specs, out_specs=out_specs, check_vma=False)
```

time: 571 us -> 128 us (0.22); the launches traced: 562 us -> 127 us
  waiting for transfers between devices: 319 us -> 3.78 us
  matrix products: 129 us -> 6.31 us
  Pallas kernels: 0 us -> 37.3 us
  between operations: 14.1 us -> 0.2 us
  other arithmetic: 18.4 us -> 5.14 us
  blocking collectives: 35.6 us -> 28.2 us
    all_gather x1 -> x0, waiting for transfers between devices: 282 us -> none  [project_table(): return lax.all_gather(own_columns, ('row', 'col'), axis=1, tiled=True)]
    dot_general x20 -> x1, matrix products: 129 us -> 6.31 us  [project_table(): lax.dot_general(w_in, normed, (((0,), (1,)), ((), ())), preferred_element...]
    pallas_call x0 -> x2, Pallas kernels: none -> 37.3 us  [the longest x1 26.8 us: local(): pl.pallas_call(signal_kernel, out_shape=(jax.ShapeDtypeStruct((rows, LANE...]
    all_to_all x2, waiting for transfers between devices: 37.3 us -> 1.57 us  [the longest x1 1.57 us: local(): lax.all_to_all(jnp.broadcast_to(token_ids[None], (devices, positions)), A...]
    all_to_all x1, blocking collectives: 35.6 us -> 28.2 us  [local(): lax.all_to_all(sent_out, AXES, split_axis=0, concat_axis=0, tiled=True)]
    all_to_all x2 -> x0, local copies, waits for them, and re-layouts: 6.15 us -> none  [the longest x1 3.12 us: local(): lax.all_to_all(signal, ('row', 'col'), split_axis=1, concat_axis=0, tiled...]
    mul x2 -> x0, local copies, waits for them, and re-layouts: 6.03 us -> none  [the longest x1 3.13 us: local_causal(): return (summed * (1.0 / total_len)).reshape(seq_len, width)]
    convert_element_type x2 -> x0, other arithmetic: 5.9 us -> none  [the longest x1 5.02 us: local(): return mixed_out.astype(jnp.bfloat16)]
  transfers between devices with their start and end apart: 4 -> 5, of which waited for: 3 -> 3; matrix products, arithmetic and copies ran while one was open for 8% -> 14% of each run, Pallas kernels for 0% -> 21%
where the time goes in v1:
time: 128 us; the launch traced here: 127 us
  Pallas kernels  37.3 us (29%)
  blocking collectives  28.2 us (22%)
  starting transfers between devices  27.8 us (22%)
  local copies, waits for them, and re-layouts  18.5 us (14%)
  matrix products  6.31 us (5%)
  other arithmetic  5.14 us (4%)
  waiting for transfers between devices  3.78 us (3%)
    all_to_all x1, blocking collectives, local(): lax.all_to_all(sent_out, AXES, split_axis=0, concat_axis=0, tiled=True)  28.2 us
    pallas_call x1, Pallas kernels, local(): pl.pallas_call(signal_kernel, out_shape=(jax.ShapeDtypeStruct((rows, LANE...  26.8 us
    unnamed x27, local copies, waits for them, and re-layouts  11.4 us
    all_to_all x1, starting transfers between devices, local(): lax.all_to_all(jnp.broadcast_to(token_ids[None], (devices, positions)), A...  11.1 us
    pallas_call x1, Pallas kernels, local(): pl.pallas_call(long_kernel, out_shape=jax.ShapeDtypeStruct((rows, LANES),...  10.5 us
    ppermute x3, starting transfers between devices, local(): lax.ppermute(own[j * width:(j + 1) * width], AXES, [(d, (3 * d + j) % dev...  8.49 us
    all_to_all x1, starting transfers between devices, local(): lax.all_to_all(sent_filter, AXES, split_axis=0, concat_axis=0, tiled=True)  8.19 us
    dot_general x1, matrix products, project_table(): lax.dot_general(w_in, normed, (((0,), (1,)), ((), ())), preferred_element...  6.31 us
  transfers between devices with their start and end apart: 5, of which 3 were waited for; matrix products, arithmetic and copies ran while one was open for 14% of the time, Pallas kernels for 21%

profile of v1, /device:TPU:0, one launch (start us, length us, event | category | flops | bytes accessed | tf_op | source)
XLA Modules:
  0.0 127.2 jit_solution(12074600829389532401)
XLA Ops:
  0.0 0.0 copy-start
  0.0 0.0 copy-start.12
  0.0 1.4 %broadcast_in_dim.4 = s32[128,1,128]{2,1,0:T(1,128)} broadcast(s32[128]{0:T(128)} %param.12), dimensions={2} | broadcast | bytes 66048 | tf_op jit(solution)/shard_map/broadcast_in_dim | solution.py:154
  1.4 11.1 %all-to-all-start.1 = ((s32[128,1,128]{2,1,0:T(1,128)}), s32[128,1,128]{2,1,0:T(1,128)S(1)}, u32[]{:S(2)}, u32[]{:S(2)}) async-start(s32[128,1,128]{2,1,0:T(1,128)} %broadcast_in_dim.4), calls=%async_computation.1 | async-start | bytes 131072 | tf_op jit(solution)/shard_map/all_to_all | solution.py:153
  12.6 5.1 %fusion = f32[512]{0:T(512)S(1)} fusion(bf16[512,8192]{1,0:T(8,128)(2,1)} %param.13), kind=kLoop, calls=%fused_computation.2 | loop fusion | flops 12582400 | bytes 8390656 | tf_op jit(solution)/shard_map/reduce_sum | solution.py:34
  17.7 0.0 copy-done.12
  17.7 2.5 %copy.21 = bf16[128,4096]{0,1:T(8,128)(2,1)} copy(f32[128,4096]{1,0:T(8,128)} %param.17) | data formatting | bytes 3145728 | tf_op args[5]
  20.3 1.6 %all-to-all-done.1 = s32[128,1,128]{2,1,0:T(1,128)S(1)} async-done(((s32[128,1,128]{2,1,0:T(1,128)}), s32[128,1,128]{2,1,0:T(1,128)S(1)}, u32[]{:S(2)}, u32[]{:S(2)}) %all-to-all-start.1) | async-done | bytes 65568 | tf_op jit(solution)/shard_map/all_to_all | solution.py:153
  21.8 8.2 %all-to-all-start = ((bf16[128,32,128]{2,1,0:T(8,128)(2,1)}), bf16[128,32,128]{2,1,0:T(8,128)(2,1)S(1)}, u32[]{:S(2)}, u32[]{:S(2)}) async-start(bf16[128,32,128]{2,1,0:T(8,128)(2,1)} %bitcast.30), calls=%async_computation | async-start | bytes 2097152 | tf_op jit(solution)/shard_map/all_to_all | solution.py:152
  30.0 0.0 copy-done
  30.1 0.0 copy-start.7
  30.1 0.0 copy-start.8
  30.1 0.0 copy-start.9
  30.1 0.0 copy-start.10
  30.1 0.0 copy-start.11
  30.1 6.3 %fusion.10 = bf16[96,512]{1,0:T(8,128)(2,1)S(1)} fusion(bf16[8192,96]{0,1:T(8,128)(2,1)S(1)} %copy-done, bf16[512,8192]{1,0:T(8,128)(2,1)} %param.13, f32[8192]{0:T(1024)S(1)} %convert_element_type.20, f32[512]{0:T(512)S(1)} %add_rsqrt_fusion), kind=kOutput, calls=%fused_computation.9 | convolution fusion | flops 822132736 | bytes 10094592 | tf_op jit(solution)/shard_map/dot_general | solution.py:36
  36.4 0.7 collective-permute-start
  37.1 7.2 %collective-permute-start.2 = (bf16[32,512]{1,0:T(8,128)(2,1)S(1)}, bf16[32,512]{1,0:T(8,128)(2,1)S(1)}, u32[]{:S(2)}, u32[]{:S(2)}) collective-permute-start(bf16[32,512]{1,0:T(8,128)(2,1)S(1)} %get-tuple-element.15), channel_id=1, source_target_pairs={{0,2},{1,5},{2,8},{3,11},{4,14},{5,17},{6,20},{7,23},{8,26},{9,29}... | collective-permute-start | bytes 98312 | tf_op jit(solution)/shard_map/ppermute | solution.py:160
  44.4 0.6 collective-permute-start.1
  45.0 2.5 %reshape.36 = f32[7,3,128,32]{3,2,1,0:T(8,128)} reshape(f32[7,12288]{1,0:T(8,128)} %param.16) | data formatting | bytes 688128 | tf_op jit(solution)/shard_map/reshape | solution.py:167
  47.5 0.9 constant_dynamic-slice_fusion
  48.4 0.8 dynamic-slice_bitcast_fusion.3
  49.1 0.1 copy.23.skip_ref
  49.2 0.1 copy.22
  49.3 0.0 collective-permute-done
  49.3 1.1 collective-permute-done.2
  50.4 1.1 collective-permute-done.1
  51.6 0.0 copy-done.7
  51.6 0.0 copy-done.8
  51.6 0.0 copy-done.9
  51.6 26.8 %signal_spectrum.1 = (f32[4096,128]{1,0:T(8,128)S(1)}, f32[4096,128]{1,0:T(8,128)S(1)}, bf16[4096,256]{1,0:T(8,128)(2,1)S(1)}) custom-call(s32[128,128]{1,0:T(8,128)S(1)} %bitcast.28, bf16[96,512]{1,0:T(8,128)(2,1)S(1)} %pad_maximum_fusion.1.table_ref, f32[96,7]{1,0:T(8,128)S(1)} %bitcast.29, bf16[256,128]{1,0:T(8,128)(2,1)S(1)} %copy-done.9, ...), custom_call_target="tpu_custom_call" | custom-call | tf_op jit(solution)/shard_map/signal_spectrum/pallas_call | solution.py:172
  78.4 0.0 copy-start.1
  78.4 1.3 %copy-done.1 = f32[4096,128]{1,0:T(8,128)} copy-done((f32[4096,128]{1,0:T(8,128)}, f32[4096,128]{1,0:T(8,128)S(1)}, u32[]{:S(2)}) %copy-start.1) | copy-done | bytes 2097176
  79.7 0.0 copy-start.3
  79.7 1.4 %copy-done.3 = f32[4096,128]{1,0:T(8,128)} copy-done((f32[4096,128]{1,0:T(8,128)}, f32[4096,128]{1,0:T(8,128)S(1)}, u32[]{:S(2)}) %copy-start.3) | copy-done | bytes 2097176
  81.1 0.0 copy-start.5
  81.1 1.3 %copy-done.5 = bf16[4096,256]{1,0:T(8,128)(2,1)} copy-done((bf16[4096,256]{1,0:T(8,128)(2,1)}, bf16[4096,256]{1,0:T(8,128)(2,1)S(1)}, u32[]{:S(2)}) %copy-start.5) | copy-done | bytes 2097176
  82.4 0.0 all-to-all-done
  82.4 0.0 copy-done.10
  82.4 0.0 copy-done.11
  82.4 0.0 copy-start.2
  82.4 1.6 %copy-done.2 = f32[4096,128]{1,0:T(8,128)S(1)} copy-done((f32[4096,128]{1,0:T(8,128)S(1)}, f32[4096,128]{1,0:T(8,128)}, u32[]{:S(2)}) %copy-start.2) | copy-done | bytes 2097176
  84.0 0.0 copy-start.4
  84.0 1.6 %copy-done.4 = f32[4096,128]{1,0:T(8,128)S(1)} copy-done((f32[4096,128]{1,0:T(8,128)S(1)}, f32[4096,128]{1,0:T(8,128)}, u32[]{:S(2)}) %copy-start.4) | copy-done | bytes 2097176
  85.6 0.0 copy-start.6
  85.6 1.6 %copy-done.6 = bf16[4096,256]{1,0:T(8,128)(2,1)S(1)} copy-done((bf16[4096,256]{1,0:T(8,128)(2,1)S(1)}, bf16[4096,256]{1,0:T(8,128)(2,1)}, u32[]{:S(2)}) %copy-start.6) | copy-done | bytes 2097176
  87.2 10.5 %long_convolution.1 = bf16[4096,128]{1,0:T(8,128)(2,1)S(1)} custom-call(bf16[4096,128]{1,0:T(8,128)(2,1)S(1)} %bitcast.26, bf16[4096,256]{1,0:T(8,128)(2,1)S(1)} %copy-done.6, f32[4096,128]{1,0:T(8,128)S(1)} %copy-done.2, f32[4096,128]{1,0:T(8,128)S(1)} %copy-done.4, f32[32,1]{1,0:T(8,128)S(1)} %copy.23.skip_ref, bf16[256,128]{1,0:T(8,128)(2,1)S(1)} %copy-done.9, ...), custom_call_target="tpu_custom_call" | custom-call | tf_op jit(solution)/shard_map/long_convolution/pallas_call | solution.py:186
  97.7 28.2 %all_to_all.18 = bf16[128,32,128]{2,1,0:T(8,128)(2,1)S(1)} all-to-all(bf16[128,32,128]{2,1,0:T(8,128)(2,1)S(1)} %bitcast.27), channel_id=1, replica_groups=mesh['row'=16,'col'=8] {'row','col'}, dimensions={0} | all-to-all | bytes 2097152 | tf_op jit(solution)/shard_map/all_to_all | solution.py:198
  125.9 1.3 %copy.24 = bf16[128,4096]{1,0:T(8,128)(2,1)} copy(bf16[128,4096]{0,1:T(8,128)(2,1)S(1)} %bitcast.31) | data formatting | bytes 2097152 | tf_op jit(solution)/shard_map/transpose | solution.py:199
  (6 shorter events, 0.1 us)
Async XLA Ops:
  0.0 30.0 %copy-start = (bf16[8192,96]{0,1:T(8,128)(2,1)S(1)}, bf16[8192,96]{0,1:T(8,128)(2,1)}, u32[]{:S(2)}) copy-start(bf16[8192,96]{0,1:T(8,128)(2,1)} %param.15) | copy-start | bytes 4718596
  0.0 17.7 %copy-start.12 = (bf16[8192]{0:T(1024)(128)(2,1)S(1)}, bf16[8192]{0:T(1024)(128)(2,1)}, u32[]{:S(2)}) copy-start(bf16[8192]{0:T(1024)(128)(2,1)} %param.14) | copy-start | bytes 49156
  1.4 20.4 %all-to-all-start.1 = ((s32[128,1,128]{2,1,0:T(1,128)}), s32[128,1,128]{2,1,0:T(1,128)S(1)}, u32[]{:S(2)}, u32[]{:S(2)}) async-start(s32[128,1,128]{2,1,0:T(1,128)} %broadcast_in_dim.4), calls=%async_computation.1 | async-start | bytes 131072 | tf_op jit(solution)/shard_map/all_to_all | solution.py:153
  21.8 60.6 %all-to-all-start = ((bf16[128,32,128]{2,1,0:T(8,128)(2,1)}), bf16[128,32,128]{2,1,0:T(8,128)(2,1)S(1)}, u32[]{:S(2)}, u32[]{:S(2)}) async-start(bf16[128,32,128]{2,1,0:T(8,128)(2,1)} %bitcast.30), calls=%async_computation | async-start | bytes 2097152 | tf_op jit(solution)/shard_map/all_to_all | solution.py:152
  30.1 21.5 %copy-start.7 = (bf16[256,256]{1,0:T(8,128)(2,1)S(1)}, bf16[256,256]{1,0:T(8,128)(2,1)}, u32[]{:S(2)}) copy-start(bf16[256,256]{1,0:T(8,128)(2,1)} %constant.65.clone.second_ref) | copy-start | bytes 393220
  30.1 21.5 %copy-start.8 = (f32[2,128,128]{2,1,0:T(8,128)S(1)}, f32[2,128,128]{2,1,0:T(8,128)}, u32[]{:S(2)}) copy-start(f32[2,128,128]{2,1,0:T(8,128)} %constant.64.clone.twist_ref) | copy-start | bytes 393220
  30.1 21.5 %copy-start.9 = (bf16[256,128]{1,0:T(8,128)(2,1)S(1)}, bf16[256,128]{1,0:T(8,128)(2,1)}, u32[]{:S(2)}) copy-start(bf16[256,128]{1,0:T(8,128)(2,1)} %constant.63.clone.first_ref) | copy-start | bytes 196612
  30.1 52.3 %copy-start.10 = (bf16[256,256]{1,0:T(8,128)(2,1)S(1)}, bf16[256,256]{1,0:T(8,128)(2,1)}, u32[]{:S(2)}) copy-start(bf16[256,256]{1,0:T(8,128)(2,1)} %constant.66.clone.second_back_ref) | copy-start | bytes 393220
  30.1 52.3 %copy-start.11 = (bf16[128,256]{1,0:T(8,128)(2,1)S(1)}, bf16[128,256]{1,0:T(8,128)(2,1)}, u32[]{:S(2)}) copy-start(bf16[128,256]{1,0:T(8,128)(2,1)} %constant.67.clone.first_back_ref) | copy-start | bytes 196612
  36.4 12.9 %collective-permute-start = (bf16[32,512]{1,0:T(8,128)(2,1)S(1)}, bf16[32,512]{1,0:T(8,128)(2,1)S(1)}, u32[]{:S(2)}, u32[]{:S(2)}) collective-permute-start(bf16[32,512]{1,0:T(8,128)(2,1)S(1)} %get-tuple-element.14), channel_id=1, source_target_pairs={{0,0},{1,3},{2,6},{3,9},{4,12},{5,15},{6,18},{7,21},{8,24},{9,27},... | collective-permute-start | bytes 98312 | tf_op jit(solution)/shard_map/ppermute | solution.py:160
  37.1 13.3 %collective-permute-start.2 = (bf16[32,512]{1,0:T(8,128)(2,1)S(1)}, bf16[32,512]{1,0:T(8,128)(2,1)S(1)}, u32[]{:S(2)}, u32[]{:S(2)}) collective-permute-start(bf16[32,512]{1,0:T(8,128)(2,1)S(1)} %get-tuple-element.15), channel_id=1, source_target_pairs={{0,2},{1,5},{2,8},{3,11},{4,14},{5,17},{6,20},{7,23},{8,26},{9,29}... | collective-permute-start | bytes 98312 | tf_op jit(solution)/shard_map/ppermute | solution.py:160
  44.4 7.2 %collective-permute-start.1 = (bf16[32,512]{1,0:T(8,128)(2,1)S(1)}, bf16[32,512]{1,0:T(8,128)(2,1)S(1)}, u32[]{:S(2)}, u32[]{:S(2)}) collective-permute-start(bf16[32,512]{1,0:T(8,128)(2,1)S(1)} %get-tuple-element.16), channel_id=1, source_target_pairs={{0,1},{1,4},{2,7},{3,10},{4,13},{5,16},{6,19},{7,22},{8,25},{9,28}... | collective-permute-start | bytes 98312 | tf_op jit(solution)/shard_map/ppermute | solution.py:160
  78.4 1.3 %copy-start.1 = (f32[4096,128]{1,0:T(8,128)}, f32[4096,128]{1,0:T(8,128)S(1)}, u32[]{:S(2)}) copy-start(f32[4096,128]{1,0:T(8,128)S(1)} %get-tuple-element.9.gate_ref) | copy-start | bytes 6291460
  79.7 1.4 %copy-start.3 = (f32[4096,128]{1,0:T(8,128)}, f32[4096,128]{1,0:T(8,128)S(1)}, u32[]{:S(2)}) copy-start(f32[4096,128]{1,0:T(8,128)S(1)} %get-tuple-element.10.signal_ref) | copy-start | bytes 6291460
  81.1 1.3 %copy-start.5 = (bf16[4096,256]{1,0:T(8,128)(2,1)}, bf16[4096,256]{1,0:T(8,128)(2,1)S(1)}, u32[]{:S(2)}) copy-start(bf16[4096,256]{1,0:T(8,128)(2,1)S(1)} %get-tuple-element.8.spectrum_ref) | copy-start | bytes 6291460
  82.4 1.6 %copy-start.2 = (f32[4096,128]{1,0:T(8,128)S(1)}, f32[4096,128]{1,0:T(8,128)}, u32[]{:S(2)}) copy-start(f32[4096,128]{1,0:T(8,128)} %copy-done.1) | copy-start | bytes 6291460
  84.0 1.6 %copy-start.4 = (f32[4096,128]{1,0:T(8,128)S(1)}, f32[4096,128]{1,0:T(8,128)}, u32[]{:S(2)}) copy-start(f32[4096,128]{1,0:T(8,128)} %copy-done.3) | copy-start | bytes 6291460
  85.6 1.6 %copy-start.6 = (bf16[4096,256]{1,0:T(8,128)(2,1)S(1)}, bf16[4096,256]{1,0:T(8,128)(2,1)}, u32[]{:S(2)}) copy-start(bf16[4096,256]{1,0:T(8,128)(2,1)} %copy-done.5) | copy-start | bytes 6291460

commit v2 on v0

v2 whole, which is shorter than its diff:
```python
import functools

import jax
import jax.numpy as jnp
import numpy as np
from jax import lax
from jax.experimental import pallas as pl
from jax.experimental.pallas import tpu as pltpu
from jax.sharding import PartitionSpec as P

AXES = ("row", "col")
EPSILON = 1e-05
LANES = 128
AT_ONCE = 32
TOGETHER = 8
F32 = jnp.float32
BF16 = jnp.bfloat16


def transform_tables(blocks, lanes):
    n = blocks * lanes
    k = np.arange(blocks)
    angle_one = 2.0 * np.pi * np.outer(4 * k + 1, np.arange(blocks)) / (4 * blocks)
    angle_twist = 2.0 * np.pi * np.outer(4 * k + 1, np.arange(lanes)) / (4 * n)
    angle_two = 2.0 * np.pi * np.outer(np.arange(lanes), np.arange(lanes)) / lanes
    first = np.concatenate([np.cos(angle_one), -np.sin(angle_one)], axis=0)
    c, s = np.cos(angle_two), np.sin(angle_two)
    second = np.block([[c, -s], [s, c]])
    second_back = np.block([[c, s], [-s, c]])
    first_back = first.T / n
    half = [x.astype(np.float32).astype(jnp.bfloat16) for x in (first, second, second_back, first_back)]
    twist = np.stack([np.cos(angle_twist), np.sin(angle_twist)]).astype(np.float32)
    return half, twist


def dot(a, b):
    return jnp.dot(a, b, preferred_element_type=F32)


def project_table(embedding, norm_gain, w_in):
    rows_f32 = embedding.astype(F32)
    inverse_rms = lax.rsqrt(jnp.mean(rows_f32 * rows_f32, axis=1, keepdims=True) + EPSILON)
    normed = (rows_f32 * inverse_rms * norm_gain.astype(F32)).astype(BF16)
    return lax.dot_general(w_in, normed, (((0,), (1,)), ((), ())), preferred_element_type=F32).astype(BF16)


def pack_kernel(filter_ref, code_ref, out_ref):
    count, rows, positions = out_ref.shape
    width = rows - 1
    turned = filter_ref[...].T
    for d in range(count):
        out_ref[d] = jnp.concatenate([turned[d * width : (d + 1) * width], code_ref[...]], axis=0).astype(BF16)


def conv_kernel(
    me_ref, arrived_ref, chunk0_ref, chunk1_ref, chunk2_ref, taps_ref, skip_ref, first_ref, twist_ref,
    second_ref, second_back_ref, first_back_ref,
    out_ref, filter_s, gate, signal, mixed, codes_s, long_s, chunks, small, *, pitch,
):
    blocks, rows_in, lanes = arrived_ref.shape
    width = rows_in - 1
    rows = 3 * width
    vocab = chunk0_ref.shape[1]
    half = vocab // 2
    tap_count = taps_ref.shape[0]
    channels = taps_ref.shape[1] // 3
    me = me_ref[0]

    share = lanes // width
    small[...] = jnp.zeros_like(small)
    for g in range(3):
        begin = pl.multiple_of(g * channels + me // share * lanes, lanes)
        small[8 * g : 8 * g + tap_count, :] = taps_ref[:, pl.ds(begin, lanes)]
    small[7:8, :] = skip_ref[pl.ds(me // share, 1), :]
    small[...] = small[...].T
    columns = small[pl.ds(pl.multiple_of(me % share * width, 8), width), :]

    chunks[0] = chunk0_ref[...]
    chunks[1] = chunk1_ref[...]
    chunks[2] = chunk2_ref[...]
    parts = [chunks[(me + g * blocks) % 3] for g in range(3)]
    folded = jnp.concatenate([x[:, :half] for x in parts] + [x[:, half:] for x in parts], axis=0)

    def cast_step(b, carry):
        got = arrived_ref[b].astype(F32)
        filter_s[pl.ds(b * pitch, width), :] = got[:width]
        codes_s[pl.ds(b, 1), :] = got[width:]
        return carry

    lax.fori_loop(0, blocks, cast_step, 0, unroll=8)
    codes_s[...] = codes_s[...].T

    def look_up(step, carry):
        found = []
        hots = []
        entry = lax.broadcasted_iota(jnp.int32, (half, blocks), 0).astype(F32) + 1.0
        for h in range(AT_ONCE):
            code = codes_s[pl.ds(AT_ONCE * step + h, 1), :]
            found.append(code)
            hots.append((entry == jnp.abs(code)).astype(F32).astype(BF16))
        both = dot(folded, jnp.concatenate(hots, axis=1))
        for h in range(AT_ONCE):
            here = both[:, h * blocks : (h + 1) * blocks]
            begin = pl.multiple_of((AT_ONCE * step + h + 8) * rows, 8)
            mixed[pl.ds(begin, rows), :] = jnp.where(found[h] < 0.0, here[rows:], here[:rows])
        return carry

    lax.fori_loop(0, lanes // AT_ONCE, look_up, 0)
    block = lax.broadcasted_iota(jnp.int32, (rows, blocks), 1)
    for i in range(1, tap_count):
        last = mixed[(lanes + 8 - i) * rows : (lanes + 9 - i) * rows, :]
        mixed[(8 - i) * rows : (9 - i) * rows, :] = jnp.where(block == 0, 0.0, pltpu.roll(last, 1, 1))

    for c in range(0, width, 8):
        taps = [
            [jnp.broadcast_to(columns[c : c + 8, 8 * g + i : 8 * g + i + 1], (8, blocks)) for i in range(tap_count)]
            for g in range(3)
        ]

        def at(p, g):
            return mixed[pl.ds(pl.multiple_of((p + 8) * rows + g * width + c, 8), 8), :]

        def filter_step(p, window):
            later = []
            total = []
            for g in range(3):
                here = at(p, g)
                value = taps[g][0] * here
                for i in range(1, tap_count):
                    value = value + taps[g][i] * window[g][i - 1]
                total.append(value)
                later.append((here,) + window[g][:-1])
            gate[pl.ds(p * pitch + c, 8), :] = total[0]
            signal[pl.ds(p * pitch + c, 8), :] = total[1] * total[2]
            return tuple(later)

        before = tuple(tuple(at(-i, g) for i in range(1, tap_count)) for g in range(3))
        lax.fori_loop(0, lanes, filter_step, before, unroll=8)

    cos = twist_ref[0]
    sin = twist_ref[1]

    def channel(ref, c):
        return ref[pl.ds(c, ref.shape[0] // pitch, stride=pitch), :]

    for begin in range(0, width, TOGETHER):
        own = range(begin, begin + TOGETHER)
        signals = [channel(signal, c).T for c in own]
        series = [x for c, s in zip(own, signals) for x in (s, channel(filter_s, c))]
        turned = []
        for j in range(0, 2 * TOGETHER, 2):
            a = dot(first_ref[...], jnp.concatenate(series[j : j + 2], axis=1).astype(BF16))
            for h in range(2):
                re = a[:blocks, h * lanes : (h + 1) * lanes]
                im = a[blocks:, h * lanes : (h + 1) * lanes]
                turned.append(jnp.concatenate([re * cos + im * sin, im * cos - re * sin], axis=1).astype(BF16))
        z = dot(jnp.concatenate(turned, axis=0), second_ref[...])
        products = []
        for h in range(TOGETHER):
            s = z[2 * h * blocks : (2 * h + 1) * blocks]
            f = z[(2 * h + 1) * blocks : (2 * h + 2) * blocks]
            s_re, s_im, f_re, f_im = s[:, :lanes], s[:, lanes:], f[:, :lanes], f[:, lanes:]
            products.append(
                jnp.concatenate([f_re * s_re - f_im * s_im, f_re * s_im + f_im * s_re], axis=1).astype(BF16)
            )
        back = dot(jnp.concatenate(products, axis=0), second_back_ref[...])
        unturned = []
        for h in range(TOGETHER):
            re = back[h * blocks : (h + 1) * blocks, :lanes]
            im = back[h * blocks : (h + 1) * blocks, lanes:]
            unturned.append(jnp.concatenate([re * cos - im * sin, im * cos + re * sin], axis=0).astype(BF16))
        for j in range(0, TOGETHER, 2):
            y = dot(first_back_ref[...], jnp.concatenate(unturned[j : j + 2], axis=1))
            for h in range(2):
                c = begin + j + h
                inner = y[:, h * lanes : (h + 1) * lanes] + columns[c : c + 1, 7:8] * signals[j + h]
                long_s[pl.ds(c, blocks, stride=pitch), :] = channel(gate, c).T * inner

    def round_step(b, carry):
        out_ref[pl.ds(pl.multiple_of(b * width, width), width), :] = long_s[pl.ds(b * pitch, width), :].astype(BF16)
        return carry

    lax.fori_loop(0, blocks, round_step, 0, unroll=8)


def local(token_ids, embedding, norm_gain, w_in, short_taps, long_filter, skip_gain):
    devices = lax.axis_size(AXES)
    me = lax.axis_index(AXES)
    positions, channels = long_filter.shape
    width = channels // devices
    vocab = embedding.shape[0]
    half = vocab // 2
    tap_count = short_taps.shape[0]
    blocks = devices
    rows = 3 * width
    (first, second, second_back, first_back), twist = transform_tables(blocks, positions)

    code = jnp.where(token_ids < half, token_ids + 1, half - 1 - token_ids).astype(F32)[None]
    steps = 8
    sent = pl.pallas_call(
        pack_kernel,
        grid=(steps,),
        in_specs=[
            pl.BlockSpec((positions, channels // steps), lambda i: (0, i)),
            pl.BlockSpec((1, positions), lambda i: (0, 0)),
        ],
        out_specs=pl.BlockSpec((devices // steps, width + 1, positions), lambda i: (i, 0, 0)),
        out_shape=jax.ShapeDtypeStruct((devices, width + 1, positions), BF16),
        name="pack",
    )(long_filter, code)
    arrived = lax.all_to_all(sent, AXES, split_axis=0, concat_axis=0, tiled=True)

    own = project_table(embedding, norm_gain, w_in)
    chunks = [
        lax.ppermute(own[j * width : (j + 1) * width], AXES, [(d, (3 * d + j) % devices) for d in range(devices)])
        for j in range(3)
    ]

    pitch = width + 1
    vmem = pl.BlockSpec(memory_space=pltpu.VMEM)
    out = pl.pallas_call(
        functools.partial(conv_kernel, pitch=pitch),
        in_specs=[pl.BlockSpec(memory_space=pltpu.SMEM)] + [vmem] * 11,
        out_specs=vmem,
        out_shape=jax.ShapeDtypeStruct((blocks * width, positions), BF16),
        scratch_shapes=[
            pltpu.VMEM((blocks * pitch, positions), F32),
            pltpu.VMEM((positions * pitch, blocks), F32),
            pltpu.VMEM((positions * pitch, blocks), F32),
            pltpu.VMEM(((positions + 8) * rows, blocks), F32),
            pltpu.VMEM((blocks, positions), F32),
            pltpu.VMEM((blocks * pitch, positions), F32),
            pltpu.VMEM((3, width, vocab), BF16),
            pltpu.VMEM((positions, positions), F32),
        ],
        compiler_params=pltpu.CompilerParams(vmem_limit_bytes=48 * 1024 * 1024),
        name="convolution",
    )(
        me[None].astype(jnp.int32), arrived, *chunks, short_taps, skip_gain.reshape(channels // LANES, LANES),
        first, twist, second, second_back, first_back,
    )

    received = lax.all_to_all(
        out.reshape(devices, width, positions), AXES, split_axis=0, concat_axis=0, tiled=True
    )
    return received.reshape(channels, positions).T


def solution(mesh):
    in_specs = (
        P(AXES),
        P(),
        P(),
        P(None, AXES),
        P(),
        P(AXES, None),
        P(),
    )
    out_specs = P(AXES, None)
    return jax.shard_map(local, mesh=mesh, in_specs=in_specs, out_specs=out_specs, check_vma=False)
```

time: 571 us -> 90 us (0.16); the launches traced: 562 us -> 89.4 us
  waiting for transfers between devices: 319 us -> 5.07 us
  matrix products: 129 us -> 3.04 us
  Pallas kernels: 0 us -> 18.1 us
  local copies, waits for them, and re-layouts: 19.3 us -> 5.01 us
  between operations: 14.1 us -> 0.12 us
  other arithmetic: 18.4 us -> 6.57 us
  blocking collectives: 35.6 us -> 29.4 us
    all_gather x1 -> x0, waiting for transfers between devices: 282 us -> none  [project_table(): return lax.all_gather(own_columns, ('row', 'col'), axis=1, tiled=True)]
    dot_general x20 -> x1, matrix products: 129 us -> 3.04 us  [project_table(): lax.dot_general(w_in, normed, (((0,), (1,)), ((), ())), preferred_element...]
    all_to_all x2 -> x1, waiting for transfers between devices: 37.3 us -> 0.01 us  [local(): lax.all_to_all(sent, AXES, split_axis=0, concat_axis=0, tiled=True)]
    pallas_call x0 -> x2, Pallas kernels: none -> 18.1 us  [the longest x1 12.3 us: local(): pl.pallas_call(functools.partial(conv_kernel, pitch=pitch), in_specs=[pl....]
    all_to_all x2 -> x1, starting transfers between devices: 22.7 us -> 11.1 us  [local(): lax.all_to_all(sent, AXES, split_axis=0, concat_axis=0, tiled=True)]
    ppermute x1 -> x3, starting transfers between devices: 3.88 us -> 11 us  [local(): lax.ppermute(own[j * width:(j + 1) * width], AXES, [(d, (3 * d + j) % dev...]
    all_to_all x1, blocking collectives: 35.6 us -> 29.4 us  [local(): lax.all_to_all(out.reshape(devices, width, positions), AXES, split_axis=0...]
    all_to_all x2 -> x0, local copies, waits for them, and re-layouts: 6.15 us -> none  [the longest x1 3.12 us: local(): lax.all_to_all(signal, ('row', 'col'), split_axis=1, concat_axis=0, tiled...]
  transfers between devices with their start and end apart: 4 -> 4, of which waited for: 3 -> 2; matrix products, arithmetic and copies ran while one was open for 8% -> 10% of each run, Pallas kernels for 0% -> 0%
where the time goes in v2:
time: 90 us; the launch traced here: 89.4 us
  blocking collectives  29.4 us (33%)
  starting transfers between devices  22.1 us (25%)
  Pallas kernels  18.1 us (20%)
  other arithmetic  6.57 us (7%)
  waiting for transfers between devices  5.07 us (6%)
  local copies, waits for them, and re-layouts  5.01 us (6%)
  matrix products  3.04 us (3%)
    all_to_all x1, blocking collectives, local(): lax.all_to_all(out.reshape(devices, width, positions), AXES, split_axis=0...  29.4 us
    pallas_call x1, Pallas kernels, local(): pl.pallas_call(functools.partial(conv_kernel, pitch=pitch), in_specs=[pl....  12.3 us
    all_to_all x1, starting transfers between devices, local(): lax.all_to_all(sent, AXES, split_axis=0, concat_axis=0, tiled=True)  11.1 us
    ppermute x3, starting transfers between devices, local(): lax.ppermute(own[j * width:(j + 1) * width], AXES, [(d, (3 * d + j) % dev...  11 us
    pallas_call x1, Pallas kernels, local(): pl.pallas_call(pack_kernel, grid=(steps,), in_specs=[pl.BlockSpec((positi...  5.79 us
    reduce_sum x1, other arithmetic, project_table(): jnp.mean(rows_f32 * rows_f32, axis=1, keepdims=True) + EPSILON  5.25 us
    ppermute x3, waiting for transfers between devices, local(): lax.ppermute(own[j * width:(j + 1) * width], AXES, [(d, (3 * d + j) % dev...  5.07 us
    unnamed x20, local copies, waits for them, and re-layouts  3.07 us
  transfers between devices with their start and end apart: 4, of which 2 were waited for; matrix products, arithmetic and copies ran while one was open for 10% of the time, Pallas kernels for 0%

profile of v2, /device:TPU:0, one launch (start us, length us, event | category | flops | bytes accessed | tf_op | source)
XLA Modules:
  0.0 89.4 jit_solution(8086582020775166724)
XLA Ops:
  0.0 0.0 copy-start
  0.0 0.0 copy-start.9
  0.0 1.3 %fusion.14.code_ref = f32[1,128]{1,0:T(1,128)} fusion(s32[128]{0:T(128)} %param.12), kind=kLoop, calls=%fused_computation.13 | loop fusion | flops 640 | bytes 1024 | tf_op jit(solution)/shard_map/broadcast_in_dim | solution.py:198
  1.3 5.8 %pack.1 = bf16[128,33,128]{2,1,0:T(8,128)(2,1)} custom-call(f32[128,4096]{1,0:T(8,128)} %filter_ref.1, f32[1,128]{1,0:T(1,128)} %fusion.14.code_ref), custom_call_target="tpu_custom_call" | custom-call | tf_op jit(solution)/shard_map/pack/pallas_call | solution.py:200
  7.1 11.1 %all-to-all-start = ((bf16[128,33,128]{2,1,0:T(8,128)(2,1)}), bf16[128,33,128]{2,1,0:T(8,128)(2,1)S(1)}, u32[]{:S(2)}, u32[]{:S(2)}) async-start(bf16[128,33,128]{2,1,0:T(8,128)(2,1)} %pack.1), calls=%async_computation | async-start | bytes 2621440 | tf_op jit(solution)/shard_map/all_to_all | solution.py:211
  18.2 0.0 copy-start.8
  18.3 5.3 %fusion = f32[512]{0:T(512)S(1)} fusion(bf16[512,8192]{1,0:T(8,128)(2,1)} %param.13), kind=kLoop, calls=%fused_computation.2 | loop fusion | flops 12582400 | bytes 8390656 | tf_op jit(solution)/shard_map/reduce_sum | solution.py:42
  23.5 0.0 copy-done.9
  23.5 0.0 copy-done
  23.5 0.5 copy-done.8
  24.0 0.0 copy-start.1
  24.0 0.0 copy-start.2
  24.0 0.0 copy-start.3
  24.0 0.0 copy-start.7
  24.0 3.0 %fusion.10 = bf16[96,512]{1,0:T(8,128)(2,1)S(1)} fusion(bf16[8192,96]{0,1:T(8,128)(2,1)S(1)} %copy-done, bf16[512,8192]{1,0:T(8,128)(2,1)S(1)} %copy-done.8, f32[8192]{0:T(1024)S(1)} %convert_element_type.20, f32[512]{0:T(512)S(1)} %add_rsqrt_fusion), kind=kOutput, calls=%fused_computation.9 | convolution fusion | flops 822132736 | bytes 10094592 | tf_op jit(solution)/shard_map/dot_general | solution.py:44
  27.1 0.6 fusion.15
  27.7 2.0 %collective-permute-start = (bf16[32,512]{1,0:T(8,128)(2,1)}, bf16[32,512]{1,0:T(8,128)(2,1)}, u32[]{:S(2)}, u32[]{:S(2)}) collective-permute-start(bf16[32,512]{1,0:T(8,128)(2,1)} %get-tuple-element.7), channel_id=1, source_target_pairs={{0,0},{1,3},{2,6},{3,9},{4,12},{5,15},{6,18},{7,21},{8,24},{9,27},... | collective-permute-start | bytes 98312 | tf_op jit(solution)/shard_map/ppermute | solution.py:215
  29.7 3.0 %collective-permute-start.1 = (bf16[32,512]{1,0:T(8,128)(2,1)}, bf16[32,512]{1,0:T(8,128)(2,1)}, u32[]{:S(2)}, u32[]{:S(2)}) collective-permute-start(bf16[32,512]{1,0:T(8,128)(2,1)} %get-tuple-element.6), channel_id=1, source_target_pairs={{0,1},{1,4},{2,7},{3,10},{4,13},{5,16},{6,19},{7,22},{8,25},{9,28}... | collective-permute-start | bytes 98312 | tf_op jit(solution)/shard_map/ppermute | solution.py:215
  32.7 6.0 %collective-permute-start.2 = (bf16[32,512]{1,0:T(8,128)(2,1)}, bf16[32,512]{1,0:T(8,128)(2,1)}, u32[]{:S(2)}, u32[]{:S(2)}) collective-permute-start(bf16[32,512]{1,0:T(8,128)(2,1)} %get-tuple-element.5), channel_id=1, source_target_pairs={{0,2},{1,5},{2,8},{3,11},{4,14},{5,17},{6,20},{7,23},{8,26},{9,29}... | collective-permute-start | bytes 98312 | tf_op jit(solution)/shard_map/ppermute | solution.py:215
  38.7 0.0 collective-permute-done.chunk0_ref
  38.7 1.6 %collective-permute-done.1.chunk1_ref = bf16[32,512]{1,0:T(8,128)(2,1)} collective-permute-done((bf16[32,512]{1,0:T(8,128)(2,1)}, bf16[32,512]{1,0:T(8,128)(2,1)}, u32[]{:S(2)}, u32[]{:S(2)}) %collective-permute-start.1) | collective-permute-done | bytes 32800 | tf_op jit(solution)/shard_map/ppermute | solution.py:215
  40.4 3.4 %collective-permute-done.2.chunk2_ref = bf16[32,512]{1,0:T(8,128)(2,1)} collective-permute-done((bf16[32,512]{1,0:T(8,128)(2,1)}, bf16[32,512]{1,0:T(8,128)(2,1)}, u32[]{:S(2)}, u32[]{:S(2)}) %collective-permute-start.2) | collective-permute-done | bytes 32800 | tf_op jit(solution)/shard_map/ppermute | solution.py:215
  43.8 0.0 all-to-all-done.arrived_ref
  43.8 0.0 copy-done.1
  43.8 0.0 copy-done.2
  43.8 0.0 copy-done.3
  43.8 0.0 copy-done.7
  43.8 0.0 copy-start.4
  43.8 0.9 %copy-done.4 = bf16[256,256]{1,0:T(8,128)(2,1)S(1)} copy-done((bf16[256,256]{1,0:T(8,128)(2,1)S(1)}, bf16[256,256]{1,0:T(8,128)(2,1)}, u32[]{:S(2)}) %copy-start.4) | copy-done | bytes 131096
  44.7 0.0 copy-start.5
  44.7 0.8 copy-done.5
  45.6 0.0 copy-start.6
  45.6 0.8 copy-done.6
  46.4 12.3 %convolution.7 = bf16[4096,128]{1,0:T(8,128)(2,1)S(1)} custom-call(s32[1]{0:T(128)} %bitcast.me_ref, bf16[128,33,128]{2,1,0:T(8,128)(2,1)S(1)} %all-to-all-done.arrived_ref, bf16[32,512]{1,0:T(8,128)(2,1)} %collective-permute-done.chunk0_ref, bf16[32,512]{1,0:T(8,128)(2,1)} %collective-permute-done.1.chunk1_ref, ...), custom_call_target="tpu_custom_call" | custom-call | tf_op jit(solution)/shard_map/convolution/pallas_call | solution.py:221
  58.7 29.4 %all_to_all.10 = bf16[128,32,128]{2,1,0:T(8,128)(2,1)S(1)} all-to-all(bf16[128,32,128]{2,1,0:T(8,128)(2,1)S(1)} %bitcast.11), channel_id=1, replica_groups=mesh['row'=16,'col'=8] {'row','col'}, dimensions={0} | all-to-all | bytes 2097152 | tf_op jit(solution)/shard_map/all_to_all | solution.py:243
  88.1 1.3 %copy.14 = bf16[128,4096]{1,0:T(8,128)(2,1)} copy(bf16[128,4096]{0,1:T(8,128)(2,1)S(1)} %bitcast.13) | data formatting | bytes 2097152 | tf_op jit(solution)/shard_map/transpose | solution.py:246
  (2 shorter events, 0.0 us)
Async XLA Ops:
  0.0 23.5 %copy-start = (bf16[8192,96]{0,1:T(8,128)(2,1)S(1)}, bf16[8192,96]{0,1:T(8,128)(2,1)}, u32[]{:S(2)}) copy-start(bf16[8192,96]{0,1:T(8,128)(2,1)} %param.15) | copy-start | bytes 4718596
  0.0 23.5 %copy-start.9 = (bf16[8192]{0:T(1024)(128)(2,1)S(1)}, bf16[8192]{0:T(1024)(128)(2,1)}, u32[]{:S(2)}) copy-start(bf16[8192]{0:T(1024)(128)(2,1)} %param.14) | copy-start | bytes 49156
  7.1 36.7 %all-to-all-start = ((bf16[128,33,128]{2,1,0:T(8,128)(2,1)}), bf16[128,33,128]{2,1,0:T(8,128)(2,1)S(1)}, u32[]{:S(2)}, u32[]{:S(2)}) async-start(bf16[128,33,128]{2,1,0:T(8,128)(2,1)} %pack.1), calls=%async_computation | async-start | bytes 2621440 | tf_op jit(solution)/shard_map/all_to_all | solution.py:211
  18.2 5.8 %copy-start.8 = (bf16[512,8192]{1,0:T(8,128)(2,1)S(1)}, bf16[512,8192]{1,0:T(8,128)(2,1)}, u32[]{:S(2)}) copy-start(bf16[512,8192]{1,0:T(8,128)(2,1)} %param.13) | copy-start | bytes 25165828
  24.0 19.8 %copy-start.1 = (f32[7,12288]{1,0:T(8,128)S(1)}, f32[7,12288]{1,0:T(8,128)}, u32[]{:S(2)}) copy-start(f32[7,12288]{1,0:T(8,128)} %taps_ref.1) | copy-start | bytes 1032196
  24.0 19.8 %copy-start.2 = (f32[2,128,128]{2,1,0:T(8,128)S(1)}, f32[2,128,128]{2,1,0:T(8,128)}, u32[]{:S(2)}) copy-start(f32[2,128,128]{2,1,0:T(8,128)} %constant.35.clone.twist_ref) | copy-start | bytes 393220
  24.0 19.8 %copy-start.3 = (bf16[256,256]{1,0:T(8,128)(2,1)S(1)}, bf16[256,256]{1,0:T(8,128)(2,1)}, u32[]{:S(2)}) copy-start(bf16[256,256]{1,0:T(8,128)(2,1)} %constant.36.clone.second_ref) | copy-start | bytes 393220
  24.0 19.8 %copy-start.7 = (f32[4096]{0:T(1024)S(1)}, f32[4096]{0:T(1024)}, u32[]{:S(2)}) copy-start(f32[4096]{0:T(1024)} %param.18) | copy-start | bytes 49156
  27.7 11.0 %collective-permute-start = (bf16[32,512]{1,0:T(8,128)(2,1)}, bf16[32,512]{1,0:T(8,128)(2,1)}, u32[]{:S(2)}, u32[]{:S(2)}) collective-permute-start(bf16[32,512]{1,0:T(8,128)(2,1)} %get-tuple-element.7), channel_id=1, source_target_pairs={{0,0},{1,3},{2,6},{3,9},{4,12},{5,15},{6,18},{7,21},{8,24},{9,27},... | collective-permute-start | bytes 98312 | tf_op jit(solution)/shard_map/ppermute | solution.py:215
  29.7 10.6 %collective-permute-start.1 = (bf16[32,512]{1,0:T(8,128)(2,1)}, bf16[32,512]{1,0:T(8,128)(2,1)}, u32[]{:S(2)}, u32[]{:S(2)}) collective-permute-start(bf16[32,512]{1,0:T(8,128)(2,1)} %get-tuple-element.6), channel_id=1, source_target_pairs={{0,1},{1,4},{2,7},{3,10},{4,13},{5,16},{6,19},{7,22},{8,25},{9,28}... | collective-permute-start | bytes 98312 | tf_op jit(solution)/shard_map/ppermute | solution.py:215
  32.7 11.1 %collective-permute-start.2 = (bf16[32,512]{1,0:T(8,128)(2,1)}, bf16[32,512]{1,0:T(8,128)(2,1)}, u32[]{:S(2)}, u32[]{:S(2)}) collective-permute-start(bf16[32,512]{1,0:T(8,128)(2,1)} %get-tuple-element.5), channel_id=1, source_target_pairs={{0,2},{1,5},{2,8},{3,11},{4,14},{5,17},{6,20},{7,23},{8,26},{9,29}... | collective-permute-start | bytes 98312 | tf_op jit(solution)/shard_map/ppermute | solution.py:215
  43.8 0.9 %copy-start.4 = (bf16[256,256]{1,0:T(8,128)(2,1)S(1)}, bf16[256,256]{1,0:T(8,128)(2,1)}, u32[]{:S(2)}) copy-start(bf16[256,256]{1,0:T(8,128)(2,1)} %constant.37.clone.second_back_ref) | copy-start | bytes 393220
  44.7 0.8 copy-start.5
  45.6 0.8 copy-start.6

commit v3 on v2

--- a/solution.py
+++ b/solution.py
@@ -28,34 +28,52 @@
     second = np.block([[c, -s], [s, c]])
     second_back = np.block([[c, s], [-s, c]])
     first_back = first.T / n
-    half = [x.astype(np.float32).astype(jnp.bfloat16) for x in (first, second, second_back, first_back)]
+    pieces = [second, second_back, first_back, np.concatenate([first[:blocks], first[blocks:]], axis=1)]
+    matrices = np.concatenate(pieces, axis=0).astype(np.float32).astype(jnp.bfloat16)
     twist = np.stack([np.cos(angle_twist), np.sin(angle_twist)]).astype(np.float32)
-    return half, twist
+    return matrices, twist
 
 
 def dot(a, b):
     return jnp.dot(a, b, preferred_element_type=F32)
 
 
-def project_table(embedding, norm_gain, w_in):
-    rows_f32 = embedding.astype(F32)
-    inverse_rms = lax.rsqrt(jnp.mean(rows_f32 * rows_f32, axis=1, keepdims=True) + EPSILON)
-    normed = (rows_f32 * inverse_rms * norm_gain.astype(F32)).astype(BF16)
-    return lax.dot_general(w_in, normed, (((0,), (1,)), ((), ())), preferred_element_type=F32).astype(BF16)
-
-
-def pack_kernel(filter_ref, code_ref, out_ref):
+def table_kernel(embedding_ref, gain_ref, w_ref, out0_ref, out1_ref, out2_ref, scaled, *, step):
+    depth = embedding_ref.shape[1]
+    width = out0_ref.shape[0]
+    for k in range(0, depth, 1024):
+        at = slice(k, k + 1024)
+        scaled[:, at] = (w_ref[:, at].astype(F32) * gain_ref[:, at].astype(F32)).astype(BF16)
+    for r in range(0, embedding_ref.shape[0], step):
+        product = lax.dot_general(
+            scaled[...], embedding_ref[r : r + step, :], (((1,), (1,)), ((), ())), preferred_element_type=F32
+        )
+        squares = jnp.zeros((step, LANES), F32)
+        for k in range(0, depth, LANES):
+            x = embedding_ref[r : r + step, k : k + LANES].astype(F32)
+            squares = squares + x * x
+        inverse_rms = lax.rsqrt(jnp.sum(squares.T, axis=0, keepdims=True) * (1.0 / depth) + EPSILON)
+        part = (product * inverse_rms).astype(BF16)
+        out0_ref[:, r : r + step] = part[:width]
+        out1_ref[:, r : r + step] = part[width : 2 * width]
+        out2_ref[:, r : r + step] = part[2 * width :]
+
+
+def pack_kernel(filter_ref, ids_ref, out_ref, *, half):
     count, rows, positions = out_ref.shape
     width = rows - 1
-    turned = filter_ref[...].T
-    for d in range(count):
-        out_ref[d] = jnp.concatenate([turned[d * width : (d + 1) * width], code_ref[...]], axis=0).astype(BF16)
+    ids = ids_ref[...]
+    code = jnp.where(ids < half, ids + 1, half - 1 - ids).astype(F32).astype(BF16)
+    group = LANES // width
+    for d in range(0, count, group):
+        turned = filter_ref[:, d * width : (d + group) * width].T.astype(BF16)
+        for e in range(group):
+            out_ref[d + e] = jnp.concatenate([turned[e * width : (e + 1) * width], code], axis=0)
 
 
 def conv_kernel(
-    me_ref, arrived_ref, chunk0_ref, chunk1_ref, chunk2_ref, taps_ref, skip_ref, first_ref, twist_ref,
-    second_ref, second_back_ref, first_back_ref,
-    out_ref, filter_s, gate, signal, mixed, codes_s, long_s, chunks, small, *, pitch,
+    me_ref, arrived_ref, chunk0_ref, chunk1_ref, chunk2_ref, taps_ref, skip_ref, matrices_ref, twist_ref, out_ref,
+    filter_s, gate, signal, mixed, codes_s, long_s, chunks, small, *, pitch,
 ):
     blocks, rows_in, lanes = arrived_ref.shape
     width = rows_in - 1
@@ -139,6 +157,12 @@
 
     cos = twist_ref[0]
     sin = twist_ref[1]
+    side = 2 * lanes
+    second = matrices_ref[:side, :]
+    second_back = matrices_ref[side : 2 * side, :]
+    first_back = matrices_ref[2 * side : 2 * side + blocks, :]
+    both_first = matrices_ref[2 * side + blocks :, :]
+    first = jnp.concatenate([both_first[:, :blocks], both_first[:, blocks:]], axis=0)
 
     def channel(ref, c):
         return ref[pl.ds(c, ref.shape[0] // pitch, stride=pitch), :]
@@ -149,12 +173,12 @@
         series = [x for c, s in zip(own, signals) for x in (s, channel(filter_s, c))]
         turned = []
         for j in range(0, 2 * TOGETHER, 2):
-            a = dot(first_ref[...], jnp.concatenate(series[j : j + 2], axis=1).astype(BF16))
+            a = dot(first, jnp.concatenate(series[j : j + 2], axis=1).astype(BF16))
             for h in range(2):
                 re = a[:blocks, h * lanes : (h + 1) * lanes]
                 im = a[blocks:, h * lanes : (h + 1) * lanes]
                 turned.append(jnp.concatenate([re * cos + im * sin, im * cos - re * sin], axis=1).astype(BF16))
-        z = dot(jnp.concatenate(turned, axis=0), second_ref[...])
+        z = dot(jnp.concatenate(turned, axis=0), second)
         products = []
         for h in range(TOGETHER):
             s = z[2 * h * blocks : (2 * h + 1) * blocks]
@@ -163,14 +187,14 @@
             products.append(
                 jnp.concatenate([f_re * s_re - f_im * s_im, f_re * s_im + f_im * s_re], axis=1).astype(BF16)
             )
-        back = dot(jnp.concatenate(products, axis=0), second_back_ref[...])
+        back = dot(jnp.concatenate(products, axis=0), second_back)
         unturned = []
         for h in range(TOGETHER):
             re = back[h * blocks : (h + 1) * blocks, :lanes]
             im = back[h * blocks : (h + 1) * blocks, lanes:]
             unturned.append(jnp.concatenate([re * cos - im * sin, im * cos + re * sin], axis=0).astype(BF16))
         for j in range(0, TOGETHER, 2):
-            y = dot(first_back_ref[...], jnp.concatenate(unturned[j : j + 2], axis=1))
+            y = dot(first_back, jnp.concatenate(unturned[j : j + 2], axis=1))
             for h in range(2):
                 c = begin + j + h
                 inner = y[:, h * lanes : (h + 1) * lanes] + columns[c : c + 1, 7:8] * signals[j + h]
@@ -183,44 +207,15 @@
     lax.fori_loop(0, blocks, round_step, 0, unroll=8)
 
 
-def local(token_ids, embedding, norm_gain, w_in, short_taps, long_filter, skip_gain):
-    devices = lax.axis_size(AXES)
-    me = lax.axis_index(AXES)
-    positions, channels = long_filter.shape
-    width = channels // devices
-    vocab = embedding.shape[0]
-    half = vocab // 2
-    tap_count = short_taps.shape[0]
-    blocks = devices
+def conv_call(me, arrived, chunk0, chunk1, chunk2, short_taps, skip_gain, matrices, twist):
+    blocks, rows_in, positions = arrived.shape
+    width, vocab = chunk0.shape
     rows = 3 * width
-    (first, second, second_back, first_back), twist = transform_tables(blocks, positions)
-
-    code = jnp.where(token_ids < half, token_ids + 1, half - 1 - token_ids).astype(F32)[None]
-    steps = 8
-    sent = pl.pallas_call(
-        pack_kernel,
-        grid=(steps,),
-        in_specs=[
-            pl.BlockSpec((positions, channels // steps), lambda i: (0, i)),
-            pl.BlockSpec((1, positions), lambda i: (0, 0)),
-        ],
-        out_specs=pl.BlockSpec((devices // steps, width + 1, positions), lambda i: (i, 0, 0)),
-        out_shape=jax.ShapeDtypeStruct((devices, width + 1, positions), BF16),
-        name="pack",
-    )(long_filter, code)
-    arrived = lax.all_to_all(sent, AXES, split_axis=0, concat_axis=0, tiled=True)
-
-    own = project_table(embedding, norm_gain, w_in)
-    chunks = [
-        lax.ppermute(own[j * width : (j + 1) * width], AXES, [(d, (3 * d + j) % devices) for d in range(devices)])
-        for j in range(3)
-    ]
-
     pitch = width + 1
     vmem = pl.BlockSpec(memory_space=pltpu.VMEM)
-    out = pl.pallas_call(
+    return pl.pallas_call(
         functools.partial(conv_kernel, pitch=pitch),
-        in_specs=[pl.BlockSpec(memory_space=pltpu.SMEM)] + [vmem] * 11,
+        in_specs=[pl.BlockSpec(memory_space=pltpu.SMEM)] + [vmem] * 8,
         out_specs=vmem,
         out_shape=jax.ShapeDtypeStruct((blocks * width, positions), BF16),
         scratch_shapes=[
@@ -233,13 +228,47 @@
             pltpu.VMEM((3, width, vocab), BF16),
             pltpu.VMEM((positions, positions), F32),
         ],
-        compiler_params=pltpu.CompilerParams(vmem_limit_bytes=48 * 1024 * 1024),
+        compiler_params=pltpu.CompilerParams(vmem_limit_bytes=32 * 1024 * 1024),
         name="convolution",
-    )(
-        me[None].astype(jnp.int32), arrived, *chunks, short_taps, skip_gain.reshape(channels // LANES, LANES),
-        first, twist, second, second_back, first_back,
-    )
-
+    )(me, arrived, chunk0, chunk1, chunk2, short_taps, skip_gain, matrices, twist)
+
+
+def local(token_ids, embedding, norm_gain, w_in, short_taps, long_filter, skip_gain):
+    devices = lax.axis_size(AXES)
+    me = lax.axis_index(AXES)
+    positions, channels = long_filter.shape
+    width = channels // devices
+    vocab = embedding.shape[0]
+    half = vocab // 2
+    blocks = devices
+    rows = 3 * width
+    matrices, twist = transform_tables(blocks, positions)
+
+    vmem = pl.BlockSpec(memory_space=pltpu.VMEM)
+    sent = pl.pallas_call(
+        functools.partial(pack_kernel, half=half),
+        in_specs=[vmem, vmem],
+        out_specs=vmem,
+        out_shape=jax.ShapeDtypeStruct((devices, width + 1, positions), BF16),
+        compiler_params=pltpu.CompilerParams(vmem_limit_bytes=8 * 1024 * 1024),
+        name="pack",
+    )(long_filter, token_ids[None])
+    arrived = lax.all_to_all(sent, AXES, split_axis=0, concat_axis=0, tiled=True)
+
+    own = pl.pallas_call(
+        functools.partial(table_kernel, step=LANES),
+        in_specs=[vmem] * 3,
+        out_specs=[vmem] * 3,
+        out_shape=[jax.ShapeDtypeStruct((width, vocab), BF16)] * 3,
+        scratch_shapes=[pltpu.VMEM((rows, embedding.shape[1]), BF16)],
+        compiler_params=pltpu.CompilerParams(vmem_limit_bytes=20 * 1024 * 1024),
+        name="table",
+    )(embedding, norm_gain[None], w_in.T)
+    chunks = [
+        lax.ppermute(own[j], AXES, [(d, (3 * d + j) % devices) for d in range(devices)]) for j in range(3)
+    ]
+
+    out = conv_call(me[None].astype(jnp.int32), arrived, *chunks, short_taps, skip_gain.reshape(channels // LANES, LANES), matrices, twist)
     received = lax.all_to_all(
         out.reshape(devices, width, positions), AXES, split_axis=0, concat_axis=0, tiled=True
     )

time: 90 us -> 81.8 us (0.909)
  other arithmetic: 6.57 us -> 0 us
  matrix products: 3.04 us -> 0 us
  local copies, waits for them, and re-layouts: 5.01 us -> 7.96 us
  Pallas kernels: 18.1 us -> 17.2 us
    reduce_sum x1 -> x0, other arithmetic: 5.25 us -> none  [project_table(): jnp.mean(rows_f32 * rows_f32, axis=1, keepdims=True) + EPSILON]
    unnamed x20 -> x18, local copies, waits for them, and re-layouts: 3.07 us -> 6.63 us
    dot_general x1 -> x0, matrix products: 3.04 us -> none  [project_table(): lax.dot_general(w_in, normed, (((0,), (1,)), ((), ())), preferred_element...]
    broadcast_in_dim x1 -> x0, other arithmetic: 1.3 us -> none  [local(): jnp.where(token_ids < half, token_ids + 1, half - 1 - token_ids).astype(F32)]
    pallas_call x2 -> x3, Pallas kernels: 18.1 us -> 17.2 us  [the longest x1 11.6 us: conv_call(): pl.pallas_call(functools.partial(conv_kernel, pitch=pitch), in_specs=[pl....]
  transfers between devices with their start and end apart: 4 -> 4, of which waited for: 2 -> 2; matrix products, arithmetic and copies ran while one was open for 10% -> 0% of each run, Pallas kernels for 0% -> 5%
where the time goes in v3:
time: 81.8 us; the launch traced here: 81.5 us
  blocking collectives  29.3 us (36%)
  starting transfers between devices  22.1 us (27%)
  Pallas kernels  17.2 us (21%)
  local copies, waits for them, and re-layouts  7.96 us (10%)
  waiting for transfers between devices  4.75 us (6%)
    all_to_all x1, blocking collectives, local(): lax.all_to_all(out.reshape(devices, width, positions), AXES, split_axis=0...  29.3 us
    pallas_call x1, Pallas kernels, conv_call(): pl.pallas_call(functools.partial(conv_kernel, pitch=pitch), in_specs=[pl....  11.6 us
    all_to_all x1, starting transfers between devices, local(): lax.all_to_all(sent, AXES, split_axis=0, concat_axis=0, tiled=True)  11.1 us
    ppermute x3, starting transfers between devices, local(): lax.ppermute(own[j], AXES, [(d, (3 * d + j) % devices) for d in range(dev...  11 us
    unnamed x18, local copies, waits for them, and re-layouts  6.63 us
    ppermute x3, waiting for transfers between devices, local(): lax.ppermute(own[j], AXES, [(d, (3 * d + j) % devices) for d in range(dev...  4.75 us
    pallas_call x1, Pallas kernels, local(): pl.pallas_call(functools.partial(table_kernel, step=LANES), in_specs=[vme...  4.13 us
  transfers between devices with their start and end apart: 4, of which 2 were waited for; matrix products, arithmetic and copies ran while one was open for 0% of the time, Pallas kernels for 5%

profile of v3, /device:TPU:0, one launch (start us, length us, event | category | flops | bytes accessed | tf_op | source)
XLA Modules:
  0.0 81.5 jit_solution(12334071931559625899)
XLA Ops:
  0.0 0.0 copy-start.1
  0.0 1.6 %copy-done.1 = f32[128,4096]{1,0:T(8,128)S(1)} copy-done((f32[128,4096]{1,0:T(8,128)S(1)}, f32[128,4096]{1,0:T(8,128)}, u32[]{:S(2)}) %copy-start.1) | copy-done | bytes 2097176
  1.6 0.0 copy-start.7
  1.6 0.7 copy-done.7
  2.2 1.4 %pack.1 = bf16[128,33,128]{2,1,0:T(8,128)(2,1)} custom-call(f32[128,4096]{1,0:T(8,128)S(1)} %copy-done.1, s32[1,128]{1,0:T(1,128)S(1)} %bitcast.11), custom_call_target="tpu_custom_call" | custom-call | tf_op jit(solution)/shard_map/pack/pallas_call | solution.py:248
  3.7 0.0 copy-start.8
  3.7 0.0 copy-start.2
  3.7 11.1 %all-to-all-start = ((bf16[128,33,128]{2,1,0:T(8,128)(2,1)}), bf16[128,33,128]{2,1,0:T(8,128)(2,1)S(1)}, u32[]{:S(2)}, u32[]{:S(2)}) async-start(bf16[128,33,128]{2,1,0:T(8,128)(2,1)} %pack.1), calls=%async_computation | async-start | bytes 2621440 | tf_op jit(solution)/shard_map/all_to_all | solution.py:256
  14.8 0.0 copy-done.8
  14.9 0.0 copy-done.2
  14.9 0.0 copy-start
  14.9 3.4 %copy-done = bf16[512,8192]{1,0:T(8,128)(2,1)S(1)} copy-done((bf16[512,8192]{1,0:T(8,128)(2,1)S(1)}, bf16[512,8192]{1,0:T(8,128)(2,1)}, u32[]{:S(2)}) %copy-start) | copy-done | bytes 8388632
  18.3 0.0 copy-start.3
  18.3 0.0 copy-start.5
  18.3 0.0 copy-start.6
  18.3 4.1 %table.1 = (bf16[32,512]{1,0:T(8,128)(2,1)S(1)}, bf16[32,512]{1,0:T(8,128)(2,1)S(1)}, bf16[32,512]{1,0:T(8,128)(2,1)S(1)}) custom-call(bf16[512,8192]{1,0:T(8,128)(2,1)S(1)} %copy-done, bf16[1,8192]{1,0:T(2,128)(2,1)S(1)} %broadcast_in_dim.11.gain_ref, bf16[96,8192]{1,0:T(8,128)(2,1)S(1)} %bitcast.9), custom_call_target="tpu_custom_call" | custom-call | tf_op jit(solution)/shard_map/table/pallas_call | solution.py:258
  22.4 0.7 collective-permute-start
  23.1 4.4 %collective-permute-start.1 = (bf16[32,512]{1,0:T(8,128)(2,1)S(1)}, bf16[32,512]{1,0:T(8,128)(2,1)S(1)}, u32[]{:S(2)}, u32[]{:S(2)}) collective-permute-start(bf16[32,512]{1,0:T(8,128)(2,1)S(1)} %get-tuple-element.9), channel_id=1, source_target_pairs={{0,1},{1,4},{2,7},{3,10},{4,13},{5,16},{6,19},{7,22},{8,25},{9,28}... | collective-permute-start | bytes 98312 | tf_op jit(solution)/shard_map/ppermute | solution.py:268
  27.4 6.0 %collective-permute-start.2 = (bf16[32,512]{1,0:T(8,128)(2,1)S(1)}, bf16[32,512]{1,0:T(8,128)(2,1)S(1)}, u32[]{:S(2)}, u32[]{:S(2)}) collective-permute-start(bf16[32,512]{1,0:T(8,128)(2,1)S(1)} %get-tuple-element.10), channel_id=1, source_target_pairs={{0,2},{1,5},{2,8},{3,11},{4,14},{5,17},{6,20},{7,23},{8,26},{9,29}... | collective-permute-start | bytes 98312 | tf_op jit(solution)/shard_map/ppermute | solution.py:268
  33.4 0.0 collective-permute-done.chunk0_ref
  33.4 2.2 %collective-permute-done.1.chunk1_ref = bf16[32,512]{1,0:T(8,128)(2,1)S(1)} collective-permute-done((bf16[32,512]{1,0:T(8,128)(2,1)S(1)}, bf16[32,512]{1,0:T(8,128)(2,1)S(1)}, u32[]{:S(2)}, u32[]{:S(2)}) %collective-permute-start.1) | collective-permute-done | bytes 32800 | tf_op jit(solution)/shard_map/ppermute | solution.py:268
  35.6 2.6 %collective-permute-done.2.chunk2_ref = bf16[32,512]{1,0:T(8,128)(2,1)S(1)} collective-permute-done((bf16[32,512]{1,0:T(8,128)(2,1)S(1)}, bf16[32,512]{1,0:T(8,128)(2,1)S(1)}, u32[]{:S(2)}, u32[]{:S(2)}) %collective-permute-start.2) | collective-permute-done | bytes 32800 | tf_op jit(solution)/shard_map/ppermute | solution.py:268
  38.2 0.0 all-to-all-done.arrived_ref
  38.2 0.0 copy-done.3
  38.2 0.0 copy-done.5
  38.2 0.0 copy-done.6
  38.2 0.0 copy-start.4
  38.2 1.0 %copy-done.4 = bf16[768,256]{1,0:T(8,128)(2,1)S(1)} copy-done((bf16[768,256]{1,0:T(8,128)(2,1)S(1)}, bf16[768,256]{1,0:T(8,128)(2,1)}, u32[]{:S(2)}) %copy-start.4) | copy-done | bytes 393240
  39.2 11.6 %convolution.1 = bf16[4096,128]{1,0:T(8,128)(2,1)S(1)} custom-call(s32[1]{0:T(128)} %bitcast.me_ref, bf16[128,33,128]{2,1,0:T(8,128)(2,1)S(1)} %all-to-all-done.arrived_ref, bf16[32,512]{1,0:T(8,128)(2,1)S(1)} %collective-permute-done.chunk0_ref, bf16[32,512]{1,0:T(8,128)(2,1)S(1)} %collective-permute-done.1.chunk1_ref, ...), custom_call_target="tpu_custom_call" | custom-call | tf_op jit(solution)/shard_map/convolution/pallas_call | solution.py:216
  50.8 29.3 %all_to_all.10 = bf16[128,32,128]{2,1,0:T(8,128)(2,1)S(1)} all-to-all(bf16[128,32,128]{2,1,0:T(8,128)(2,1)S(1)} %bitcast.8), channel_id=1, replica_groups=mesh['row'=16,'col'=8] {'row','col'}, dimensions={0} | all-to-all | bytes 2097152 | tf_op jit(solution)/shard_map/all_to_all | solution.py:272
  80.2 1.3 %copy.11 = bf16[128,4096]{1,0:T(8,128)(2,1)} copy(bf16[128,4096]{0,1:T(8,128)(2,1)S(1)} %bitcast.12) | data formatting | bytes 2097152 | tf_op jit(solution)/shard_map/transpose | solution.py:275
  (1 shorter events, 0.0 us)
Async XLA Ops:
  0.0 1.6 %copy-start.1 = (f32[128,4096]{1,0:T(8,128)S(1)}, f32[128,4096]{1,0:T(8,128)}, u32[]{:S(2)}) copy-start(f32[128,4096]{1,0:T(8,128)} %filter_ref.1) | copy-start | bytes 6291460
  1.6 0.7 copy-start.7
  3.7 11.2 %copy-start.8 = (bf16[8192]{0:T(1024)(128)(2,1)S(1)}, bf16[8192]{0:T(1024)(128)(2,1)}, u32[]{:S(2)}) copy-start(bf16[8192]{0:T(1024)(128)(2,1)} %param.11) | copy-start | bytes 49156
  3.7 11.2 %copy-start.2 = (bf16[8192,96]{0,1:T(8,128)(2,1)S(1)}, bf16[8192,96]{0,1:T(8,128)(2,1)}, u32[]{:S(2)}) copy-start(bf16[8192,96]{0,1:T(8,128)(2,1)} %param.12) | copy-start | bytes 4718596
  3.7 34.5 %all-to-all-start = ((bf16[128,33,128]{2,1,0:T(8,128)(2,1)}), bf16[128,33,128]{2,1,0:T(8,128)(2,1)S(1)}, u32[]{:S(2)}, u32[]{:S(2)}) async-start(bf16[128,33,128]{2,1,0:T(8,128)(2,1)} %pack.1), calls=%async_computation | async-start | bytes 2621440 | tf_op jit(solution)/shard_map/all_to_all | solution.py:256
  14.9 3.4 %copy-start = (bf16[512,8192]{1,0:T(8,128)(2,1)S(1)}, bf16[512,8192]{1,0:T(8,128)(2,1)}, u32[]{:S(2)}) copy-start(bf16[512,8192]{1,0:T(8,128)(2,1)} %embedding_ref.1) | copy-start | bytes 25165828
  18.3 19.9 %copy-start.3 = (f32[7,12288]{1,0:T(8,128)S(1)}, f32[7,12288]{1,0:T(8,128)}, u32[]{:S(2)}) copy-start(f32[7,12288]{1,0:T(8,128)} %taps_ref.1) | copy-start | bytes 1032196
  18.3 19.9 %copy-start.5 = (f32[2,128,128]{2,1,0:T(8,128)S(1)}, f32[2,128,128]{2,1,0:T(8,128)}, u32[]{:S(2)}) copy-start(f32[2,128,128]{2,1,0:T(8,128)} %constant.16.clone.twist_ref) | copy-start | bytes 393220
  18.3 19.9 %copy-start.6 = (f32[4096]{0:T(1024)S(1)}, f32[4096]{0:T(1024)}, u32[]{:S(2)}) copy-start(f32[4096]{0:T(1024)} %param.15) | copy-start | bytes 49156
  22.4 11.0 %collective-permute-start = (bf16[32,512]{1,0:T(8,128)(2,1)S(1)}, bf16[32,512]{1,0:T(8,128)(2,1)S(1)}, u32[]{:S(2)}, u32[]{:S(2)}) collective-permute-start(bf16[32,512]{1,0:T(8,128)(2,1)S(1)} %get-tuple-element.8), channel_id=1, source_target_pairs={{0,0},{1,3},{2,6},{3,9},{4,12},{5,15},{6,18},{7,21},{8,24},{9,27},... | collective-permute-start | bytes 98312 | tf_op jit(solution)/shard_map/ppermute | solution.py:268
  23.1 12.5 %collective-permute-start.1 = (bf16[32,512]{1,0:T(8,128)(2,1)S(1)}, bf16[32,512]{1,0:T(8,128)(2,1)S(1)}, u32[]{:S(2)}, u32[]{:S(2)}) collective-permute-start(bf16[32,512]{1,0:T(8,128)(2,1)S(1)} %get-tuple-element.9), channel_id=1, source_target_pairs={{0,1},{1,4},{2,7},{3,10},{4,13},{5,16},{6,19},{7,22},{8,25},{9,28}... | collective-permute-start | bytes 98312 | tf_op jit(solution)/shard_map/ppermute | solution.py:268
  27.4 10.7 %collective-permute-start.2 = (bf16[32,512]{1,0:T(8,128)(2,1)S(1)}, bf16[32,512]{1,0:T(8,128)(2,1)S(1)}, u32[]{:S(2)}, u32[]{:S(2)}) collective-permute-start(bf16[32,512]{1,0:T(8,128)(2,1)S(1)} %get-tuple-element.10), channel_id=1, source_target_pairs={{0,2},{1,5},{2,8},{3,11},{4,14},{5,17},{6,20},{7,23},{8,26},{9,29}... | collective-permute-start | bytes 98312 | tf_op jit(solution)/shard_map/ppermute | solution.py:268
  38.2 1.0 %copy-start.4 = (bf16[768,256]{1,0:T(8,128)(2,1)S(1)}, bf16[768,256]{1,0:T(8,128)(2,1)}, u32[]{:S(2)}) copy-start(bf16[768,256]{1,0:T(8,128)(2,1)} %constant.15.clone.matrices_ref) | copy-start | bytes 1179652

commit v4 on v3

v4 whole, which is shorter than its diff:
```python
import functools

import jax
import jax.numpy as jnp
import numpy as np
from jax import lax
from jax.experimental import pallas as pl
from jax.experimental.pallas import tpu as pltpu
from jax.sharding import PartitionSpec as P

AXES = ("row", "col")
EPSILON = 1e-05
LANES = 128
AT_ONCE = 32
PACK_VMEM = 62
TABLE_VMEM = 20
TOGETHER = 8
F32 = jnp.float32
BF16 = jnp.bfloat16


def transform_tables(blocks, lanes):
    n = blocks * lanes
    k = np.arange(blocks)
    angle_one = 2.0 * np.pi * np.outer(4 * k + 1, np.arange(blocks)) / (4 * blocks)
    angle_twist = 2.0 * np.pi * np.outer(4 * k + 1, np.arange(lanes)) / (4 * n)
    angle_two = 2.0 * np.pi * np.outer(np.arange(lanes), np.arange(lanes)) / lanes
    one = np.concatenate([np.cos(angle_one), -np.sin(angle_one)], axis=1)
    two = np.concatenate([np.cos(angle_two), np.sin(angle_two)], axis=1)
    back = np.concatenate([np.cos(angle_one).T, -np.sin(angle_one).T], axis=1) / n
    rounded = np.concatenate([one, two, back], axis=0).astype(np.float32).astype(jnp.bfloat16).astype(np.float32)
    twist = np.concatenate([np.cos(angle_twist), np.sin(angle_twist)], axis=1).astype(np.float32)
    return np.concatenate([twist, rounded], axis=0)


def dot(a, b):
    return jnp.dot(a, b, preferred_element_type=F32)


def table_kernel(
    me_ref, embedding_ref, gain_ref, w_ref, taps_hbm, skip_hbm, out0_ref, out1_ref, out2_ref, columns_ref,
    normed, gain_wide, small, small_arrived,
):
    vocab, depth = embedding_ref.shape
    width = out0_ref.shape[0]
    tap_count = taps_hbm.shape[0]
    channels = taps_hbm.shape[1] // 3
    share = LANES // width
    me = me_ref[0]
    few = [pltpu.make_async_copy(skip_hbm.at[pl.ds(me // share, 1), :], small.at[pl.ds(24, 1), :], small_arrived.at[3])]
    for g in range(3):
        at = pl.ds(pl.multiple_of(g * channels + me // share * LANES, LANES), LANES)
        few.append(
            pltpu.make_async_copy(taps_hbm.at[:, at], small.at[pl.ds(8 * g, tap_count), :], small_arrived.at[g])
        )
    for copy in few:
        copy.start()
    gain_wide[...] = jnp.broadcast_to(gain_ref[...].astype(F32), gain_wide.shape)
    for copy in few:
        copy.wait()
    small[...] = small[...].T
    columns_ref[...] = small[pl.ds(pl.multiple_of(me % share * width, 8), width), :]

    @pl.loop(0, vocab // LANES)
    def _(part):
        begin = pl.multiple_of(part * LANES, LANES)

        def norm_step(i, carry):
            x = embedding_ref[pl.ds(pl.multiple_of(begin + i * 16, 16), 16), :].astype(F32)
            inverse_rms = lax.rsqrt(jnp.mean(x * x, axis=1, keepdims=True) + EPSILON)
            gain = jnp.concatenate([gain_wide[...]] * 2, axis=0)
            normed[pl.ds(pl.multiple_of(i * 16, 16), 16), :] = (x * inverse_rms * gain).astype(BF16)
            return carry

        lax.fori_loop(0, LANES // 16, norm_step, 0, unroll=8)
        product = lax.dot_general(
            w_ref[...], normed[...], (((1,), (1,)), ((), ())), preferred_element_type=F32
        ).astype(BF16)
        for j, out_ref in enumerate((out0_ref, out1_ref, out2_ref)):
            out_ref[:, pl.ds(begin, LANES)] = product[j * width : (j + 1) * width]


def pack_kernel(filter_hbm, ids_hbm, out_ref, filter_ref, ids_ref, arrived, *, half):
    count, rows, positions = out_ref.shape
    width = rows - 1
    group = LANES // width
    part = filter_hbm.shape[1] // 4
    copies = [pltpu.make_async_copy(ids_hbm, ids_ref, arrived.at[4])]
    for k in range(4):
        at = pl.ds(k * part, part)
        copies.append(pltpu.make_async_copy(filter_hbm.at[:, at], filter_ref.at[:, at], arrived.at[k]))
    for copy in copies:
        copy.start()
    copies[0].wait()
    ids = ids_ref[...]
    code = jnp.where(ids < half, ids + 1, half - 1 - ids).astype(F32).astype(BF16)
    inverse = pow(3, -1, count)
    for q in range(0, count, group):
        if q * width % part == 0:
            copies[1 + q * width // part].wait()
        turned = filter_ref[:, q * width : (q + group) * width].T.astype(BF16)
        for e in range(group):
            out_ref[(q + e) * inverse % count] = jnp.concatenate(
                [turned[e * width : (e + 1) * width], code], axis=0
            )


def unpack_kernel(received_ref, out_ref):
    count, width, positions = received_ref.shape
    inverse = pow(3, -1, count)
    group = LANES // width
    for q in range(0, count, group):
        rows = [received_ref[(q + e) * inverse % count].astype(F32) for e in range(group)]
        out_ref[:, q * width : (q + group) * width] = jnp.concatenate(rows, axis=0).T.astype(BF16)


def matrices(constants_ref):
    lanes = LANES
    blocks = (constants_ref.shape[0] - lanes) // 3
    cos = constants_ref[:blocks, :lanes]
    sin = constants_ref[:blocks, lanes:]
    one = constants_ref[blocks : 2 * blocks, :].astype(BF16)
    first = jnp.concatenate([one[:, :blocks], one[:, blocks:]], axis=0)
    two = constants_ref[2 * blocks : 2 * blocks + lanes, :]
    real, imaginary = two[:, :lanes].astype(BF16), two[:, lanes:].astype(BF16)
    minus = (-two[:, lanes:]).astype(BF16)
    second = jnp.concatenate(
        [jnp.concatenate([real, minus], axis=1), jnp.concatenate([imaginary, real], axis=1)], axis=0
    )
    second_back = jnp.concatenate(
        [jnp.concatenate([real, imaginary], axis=1), jnp.concatenate([minus, real], axis=1)], axis=0
    )
    first_back = constants_ref[2 * blocks + lanes :, :].astype(BF16)
    return cos, sin, first, second, second_back, first_back


def channel(ref, c, pitch):
    return ref[pl.ds(c, ref.shape[0] // pitch, stride=pitch), :]


def forward(series, cos, sin, first, second):
    blocks, lanes = cos.shape
    turned = []
    for j in range(0, len(series), 2):
        a = dot(first, jnp.concatenate(series[j : j + 2], axis=1).astype(BF16))
        for h in range(2):
            re = a[:blocks, h * lanes : (h + 1) * lanes]
            im = a[blocks:, h * lanes : (h + 1) * lanes]
            turned.append(jnp.concatenate([re * cos + im * sin, im * cos - re * sin], axis=1).astype(BF16))
    return dot(jnp.concatenate(turned, axis=0), second)


def filter_kernel(arrived_ref, constants_ref, spectrum_ref, codes_ref, filter_s, *, pitch):
    blocks, rows_in, lanes = arrived_ref.shape
    width = rows_in - 1

    def cast_step(b, carry):
        got = arrived_ref[b].astype(F32)
        filter_s[pl.ds(b * pitch, width), :] = got[:width]
        codes_ref[pl.ds(b, 1), :] = got[width:]
        return carry

    lax.fori_loop(0, blocks, cast_step, 0, unroll=8)
    codes_ref[...] = codes_ref[...].T
    cos, sin, first, second, _, _ = matrices(constants_ref)
    for c in range(0, width, TOGETHER):
        z = forward([channel(filter_s, c + h, pitch) for h in range(TOGETHER)], cos, sin, first, second)
        spectrum_ref[c * blocks : (c + TOGETHER) * blocks, :] = z.astype(BF16)


def conv_kernel(
    me_ref, spectrum_ref, codes_s, chunk0_ref, chunk1_ref, chunk2_ref, columns_ref, constants_ref, out_ref,
    gate, signal, mixed, long_s, chunks, *, tap_count, pitch,
):
    blocks, lanes = codes_s.shape[::-1]
    width = chunk0_ref.shape[0]
    rows = 3 * width
    vocab = chunk0_ref.shape[1]
    half = vocab // 2
    me = me_ref[0]
    columns = columns_ref[...]

    chunks[0] = chunk0_ref[...]
    chunks[1] = chunk1_ref[...]
    chunks[2] = chunk2_ref[...]
    parts = [chunks[(me + g * blocks) % 3] for g in range(3)]
    folded = jnp.concatenate([x[:, :half] for x in parts] + [x[:, half:] for x in parts], axis=0)

    def look_up(step, carry):
        found = []
        hots = []
        entry = lax.broadcasted_iota(jnp.int32, (half, blocks), 0).astype(F32) + 1.0
        for h in range(AT_ONCE):
            code = codes_s[pl.ds(AT_ONCE * step + h, 1), :]
            found.append(code)
            hots.append((entry == jnp.abs(code)).astype(F32).astype(BF16))
        both = dot(folded, jnp.concatenate(hots, axis=1))
        for h in range(AT_ONCE):
            here = both[:, h * blocks : (h + 1) * blocks]
            begin = pl.multiple_of((AT_ONCE * step + h + 8) * rows, 8)
            mixed[pl.ds(begin, rows), :] = jnp.where(found[h] < 0.0, here[rows:], here[:rows])
        return carry

    lax.fori_loop(0, lanes // AT_ONCE, look_up, 0)
    block = lax.broadcasted_iota(jnp.int32, (rows, blocks), 1)
    for i in range(1, tap_count):
        last = mixed[(lanes + 8 - i) * rows : (lanes + 9 - i) * rows, :]
        mixed[(8 - i) * rows : (9 - i) * rows, :] = jnp.where(block == 0, 0.0, pltpu.roll(last, 1, 1))

    for c in range(0, width, 8):
        taps = [
            [jnp.broadcast_to(columns[c : c + 8, 8 * g + i : 8 * g + i + 1], (8, blocks)) for i in range(tap_count)]
            for g in range(3)
        ]

        def at(p, g):
            return mixed[pl.ds(pl.multiple_of((p + 8) * rows + g * width + c, 8), 8), :]

        def filter_step(p, window):
            later = []
            total = []
            for g in range(3):
                here = at(p, g)
                value = taps[g][0] * here
                for i in range(1, tap_count):
                    value = value + taps[g][i] * window[g][i - 1]
                total.append(value)
                later.append((here,) + window[g][:-1])
            gate[pl.ds(p * pitch + c, 8), :] = total[0]
            signal[pl.ds(p * pitch + c, 8), :] = total[1] * total[2]
            return tuple(later)

        before = tuple(tuple(at(-i, g) for i in range(1, tap_count)) for g in range(3))
        lax.fori_loop(0, lanes, filter_step, before, unroll=8)

    cos, sin, first, second, second_back, first_back = matrices(constants_ref)

    for begin in range(0, width, TOGETHER):
        signals = [channel(signal, begin + h, pitch).T for h in range(TOGETHER)]
        z = forward(signals, cos, sin, first, second)
        products = []
        for h in range(TOGETHER):
            s = z[h * blocks : (h + 1) * blocks]
            f = spectrum_ref[(begin + h) * blocks : (begin + h + 1) * blocks, :].astype(F32)
            s_re, s_im, f_re, f_im = s[:, :lanes], s[:, lanes:], f[:, :lanes], f[:, lanes:]
            products.append(
                jnp.concatenate([f_re * s_re - f_im * s_im, f_re * s_im + f_im * s_re], axis=1).astype(BF16)
            )
        back = dot(jnp.concatenate(products, axis=0), second_back)
        unturned = []
        for h in range(TOGETHER):
            re = back[h * blocks : (h + 1) * blocks, :lanes]
            im = back[h * blocks : (h + 1) * blocks, lanes:]
            unturned.append(jnp.concatenate([re * cos - im * sin, im * cos + re * sin], axis=0).astype(BF16))
        for j in range(0, TOGETHER, 2):
            y = dot(first_back, jnp.concatenate(unturned[j : j + 2], axis=1))
            for h in range(2):
                c = begin + j + h
                inner = y[:, h * lanes : (h + 1) * lanes] + columns[c : c + 1, 24:25] * signals[j + h]
                long_s[pl.ds(c, blocks, stride=pitch), :] = channel(gate, c, pitch).T * inner

    def round_step(b, carry):
        out_ref[pl.ds(pl.multiple_of(b * width, width), width), :] = long_s[pl.ds(b * pitch, width), :].astype(BF16)
        return carry

    lax.fori_loop(0, blocks, round_step, 0, unroll=8)


def conv_call(me, arrived, chunk0, chunk1, chunk2, columns, constants, tap_count):
    blocks, rows_in, positions = arrived.shape
    width, vocab = chunk0.shape
    rows = 3 * width
    pitch = width + 1
    vmem = pl.BlockSpec(memory_space=pltpu.VMEM)
    spectrum, codes = pl.pallas_call(
        functools.partial(filter_kernel, pitch=pitch),
        in_specs=[vmem] * 2,
        out_specs=[vmem] * 2,
        out_shape=[
            jax.ShapeDtypeStruct((width * blocks, 2 * positions), BF16),
            jax.ShapeDtypeStruct((positions, blocks), F32),
        ],
        scratch_shapes=[pltpu.VMEM((blocks * pitch, positions), F32)],
        compiler_params=pltpu.CompilerParams(vmem_limit_bytes=16 * 1024 * 1024),
        name="filter_spectrum",
    )(arrived, constants)
    return pl.pallas_call(
        functools.partial(conv_kernel, tap_count=tap_count, pitch=pitch),
        in_specs=[pl.BlockSpec(memory_space=pltpu.SMEM)] + [vmem] * 7,
        out_specs=vmem,
        out_shape=jax.ShapeDtypeStruct((blocks * width, positions), BF16),
        scratch_shapes=[
            pltpu.VMEM((positions * pitch, blocks), F32),
            pltpu.VMEM((positions * pitch, blocks), F32),
            pltpu.VMEM(((positions + 8) * rows, blocks), F32),
            pltpu.VMEM((blocks * pitch, positions), F32),
            pltpu.VMEM((3, width, vocab), BF16),
        ],
        compiler_params=pltpu.CompilerParams(vmem_limit_bytes=32 * 1024 * 1024),
        name="convolution",
    )(me, spectrum, codes, chunk0, chunk1, chunk2, columns, constants)


def local(token_ids, embedding, norm_gain, w_in, short_taps, long_filter, skip_gain):
    devices = lax.axis_size(AXES)
    me = lax.axis_index(AXES)
    positions, channels = long_filter.shape
    width = channels // devices
    vocab = embedding.shape[0]
    half = vocab // 2
    blocks = devices
    rows = 3 * width
    constants = transform_tables(blocks, positions)

    vmem = pl.BlockSpec(memory_space=pltpu.VMEM)
    hbm = pl.BlockSpec(memory_space=pltpu.HBM)
    sent = pl.pallas_call(
        functools.partial(pack_kernel, half=half),
        in_specs=[hbm, hbm],
        out_specs=vmem,
        out_shape=jax.ShapeDtypeStruct((devices, width + 1, positions), BF16),
        scratch_shapes=[
            pltpu.VMEM((positions, channels), F32),
            pltpu.VMEM((1, positions), jnp.int32),
            pltpu.SemaphoreType.DMA((5,)),
        ],
        compiler_params=pltpu.CompilerParams(vmem_limit_bytes=PACK_VMEM * 1024 * 1024),
        name="pack",
    )(long_filter, token_ids[None])
    arrived = lax.all_to_all(sent, AXES, split_axis=0, concat_axis=0, tiled=True)

    block = (3 * me % devices)[None].astype(jnp.int32)
    *own, columns = pl.pallas_call(
        table_kernel,
        in_specs=[pl.BlockSpec(memory_space=pltpu.SMEM), vmem, vmem, vmem, hbm, hbm],
        out_specs=[vmem] * 4,
        out_shape=[jax.ShapeDtypeStruct((width, vocab), BF16)] * 3 + [jax.ShapeDtypeStruct((width, LANES), F32)],
        scratch_shapes=[
            pltpu.VMEM((LANES, embedding.shape[1]), BF16),
            pltpu.VMEM((8, embedding.shape[1]), F32),
            pltpu.VMEM((LANES, LANES), F32),
            pltpu.SemaphoreType.DMA((4,)),
        ],
        compiler_params=pltpu.CompilerParams(vmem_limit_bytes=TABLE_VMEM * 1024 * 1024),
        name="table",
    )(block, embedding, norm_gain[None], w_in.T, short_taps, skip_gain.reshape(channels // LANES, LANES))
    inverse = pow(3, -1, devices)
    chunks = [own[0]] + [
        lax.ppermute(own[j], AXES, [(d, (d + j * inverse) % devices) for d in range(devices)]) for j in (1, 2)
    ]

    out = conv_call(block, arrived, *chunks, columns, constants, short_taps.shape[0])
    received = lax.all_to_all(
        out.reshape(devices, width, positions), AXES, split_axis=0, concat_axis=0, tiled=True
    )
    return pl.pallas_call(
        unpack_kernel,
        in_specs=[vmem],
        out_specs=vmem,
        out_shape=jax.ShapeDtypeStruct((positions, channels), BF16),
        compiler_params=pltpu.CompilerParams(vmem_limit_bytes=16 * 1024 * 1024),
        name="unpack",
    )(received)


def solution(mesh):
    in_specs = (
        P(AXES),
        P(),
        P(),
        P(None, AXES),
        P(),
        P(AXES, None),
        P(),
    )
    out_specs = P(AXES, None)
    return jax.shard_map(local, mesh=mesh, in_specs=in_specs, out_specs=out_specs, check_vma=False)
```

time: 81.8 us -> 74.9 us (0.916)
  starting transfers between devices: 22.1 us -> 17.5 us
  Pallas kernels: 17.2 us -> 21.7 us
  local copies, waits for them, and re-layouts: 7.96 us -> 4.41 us
  blocking collectives: 29.3 us -> 26.2 us
    ppermute x3 -> x2, waiting for transfers between devices: 4.75 us -> 0.01 us  [local(): lax.ppermute(own[j], AXES, [(d, (d + j * inverse) % devices) for d in ran...]
    all_to_all x1, waiting for transfers between devices: 0.01 us -> 4.64 us  [local(): lax.all_to_all(sent, AXES, split_axis=0, concat_axis=0, tiled=True)]
    ppermute x3 -> x2, starting transfers between devices: 11 us -> 6.4 us  [local(): lax.ppermute(own[j], AXES, [(d, (d + j * inverse) % devices) for d in ran...]
    pallas_call x3 -> x5, Pallas kernels: 17.2 us -> 21.7 us  [the longest x1 9.66 us: conv_call(): pl.pallas_call(functools.partial(conv_kernel, tap_count=tap_count, pitch=...]
    all_to_all x1, blocking collectives: 29.3 us -> 26.2 us  [local(): lax.all_to_all(out.reshape(devices, width, positions), AXES, split_axis=0...]
    unnamed x18 -> x12, local copies, waits for them, and re-layouts: 6.63 us -> 4.39 us
    transpose x1 -> x0, local copies, waits for them, and re-layouts: 1.3 us -> none  [local(): return received.reshape(channels, positions).T]
  transfers between devices with their start and end apart: 4 -> 3, of which waited for: 2 -> 1; matrix products, arithmetic and copies ran while one was open for 0% -> 0% of each run, Pallas kernels for 5% -> 11%
where the time goes in v4:
time: 74.9 us; the launch traced here: 74.6 us
  blocking collectives  26.2 us (35%)
  Pallas kernels  21.7 us (29%)
  starting transfers between devices  17.5 us (23%)
  waiting for transfers between devices  4.64 us (6%)
  local copies, waits for them, and re-layouts  4.41 us (6%)
    all_to_all x1, blocking collectives, local(): lax.all_to_all(out.reshape(devices, width, positions), AXES, split_axis=0...  26.2 us
    all_to_all x1, starting transfers between devices, local(): lax.all_to_all(sent, AXES, split_axis=0, concat_axis=0, tiled=True)  11.1 us
    pallas_call x1, Pallas kernels, conv_call(): pl.pallas_call(functools.partial(conv_kernel, tap_count=tap_count, pitch=...  9.66 us
    ppermute x2, starting transfers between devices, local(): lax.ppermute(own[j], AXES, [(d, (d + j * inverse) % devices) for d in ran...  6.4 us
    pallas_call x1, Pallas kernels, local(): pl.pallas_call(table_kernel, in_specs=[pl.BlockSpec(memory_space=pltpu.SM...  6.17 us
    all_to_all x1, waiting for transfers between devices, local(): lax.all_to_all(sent, AXES, split_axis=0, concat_axis=0, tiled=True)  4.64 us
    unnamed x12, local copies, waits for them, and re-layouts  4.39 us
    pallas_call x1, Pallas kernels, local(): pl.pallas_call(functools.partial(pack_kernel, half=half), in_specs=[hbm,...  2.8 us
  transfers between devices with their start and end apart: 3, of which 1 were waited for; matrix products, arithmetic and copies ran while one was open for 0% of the time, Pallas kernels for 11%

profile of v4, /device:TPU:0, one launch (start us, length us, event | category | flops | bytes accessed | tf_op | source)
XLA Modules:
  0.0 74.6 jit_solution(10620353031662720342)
XLA Ops:
  0.0 2.8 %pack.1 = bf16[128,33,128]{2,1,0:T(8,128)(2,1)} custom-call(f32[128,4096]{1,0:T(8,128)} %filter_hbm.1, s32[1,128]{1,0:T(1,128)} %bitcast.8), custom_call_target="tpu_custom_call" | custom-call | tf_op jit(solution)/shard_map/pack/pallas_call | solution.py:317
  2.8 0.0 copy-start.5
  2.8 0.0 copy-start.2
  2.8 0.0 copy-start.4
  2.8 11.1 %all-to-all-start = ((bf16[128,33,128]{2,1,0:T(8,128)(2,1)}), bf16[128,33,128]{2,1,0:T(8,128)(2,1)S(1)}, u32[]{:S(2)}, u32[]{:S(2)}) async-start(bf16[128,33,128]{2,1,0:T(8,128)(2,1)} %pack.1), calls=%async_computation | async-start | bytes 2621440 | tf_op jit(solution)/shard_map/all_to_all | solution.py:330
  14.0 0.0 copy-done.5
  14.1 0.0 copy-done.2
  14.1 0.0 copy-done.4
  14.1 0.0 copy-start
  14.1 3.4 %copy-done = bf16[512,8192]{1,0:T(8,128)(2,1)S(1)} copy-done((bf16[512,8192]{1,0:T(8,128)(2,1)S(1)}, bf16[512,8192]{1,0:T(8,128)(2,1)}, u32[]{:S(2)}) %copy-start) | copy-done | bytes 8388632
  17.5 0.0 copy-start.3
  17.5 1.0 %copy-done.3 = f32[7,12288]{1,0:T(8,128)S(1)} copy-done((f32[7,12288]{1,0:T(8,128)S(1)}, f32[7,12288]{1,0:T(8,128)}, u32[]{:S(2)}) %copy-start.3) | copy-done | bytes 344088
  18.5 0.0 copy-start.1
  18.5 6.2 %table.1 = (bf16[32,512]{1,0:T(8,128)(2,1)S(1)}, bf16[32,512]{1,0:T(8,128)(2,1)}, bf16[32,512]{1,0:T(8,128)(2,1)S(1)}, f32[32,128]{1,0:T(8,128)S(1)}) custom-call(s32[1]{0:T(128)} %bitcast.me_ref, bf16[512,8192]{1,0:T(8,128)(2,1)S(1)} %copy-done, bf16[1,8192]{1,0:T(2,128)(2,1)S(1)} %broadcast_in_dim.11.gain_ref, bf16[96,8192]{1,0:T(8,128)(2,1)S(1)} %bitcast.6, ...), custom_call_target="tpu_custom_call" | custom-call | tf_op jit(solution)/shard_map/table/pallas_call | solution.py:333
  24.6 4.4 %collective-permute-start = (bf16[32,512]{1,0:T(8,128)(2,1)}, bf16[32,512]{1,0:T(8,128)(2,1)S(1)}, u32[]{:S(2)}, u32[]{:S(2)}) collective-permute-start(bf16[32,512]{1,0:T(8,128)(2,1)} %get-tuple-element.14), channel_id=1, source_target_pairs={{0,43},{1,44},{2,45},{3,46},{4,47},{5,48},{6,49},{7,50},{8,51},{9,... | collective-permute-start | bytes 98312 | tf_op jit(solution)/shard_map/ppermute | solution.py:349
  29.1 2.0 %collective-permute-start.1 = (bf16[32,512]{1,0:T(8,128)(2,1)S(1)}, bf16[32,512]{1,0:T(8,128)(2,1)S(1)}, u32[]{:S(2)}, u32[]{:S(2)}) collective-permute-start(bf16[32,512]{1,0:T(8,128)(2,1)S(1)} %get-tuple-element.15), channel_id=1, source_target_pairs={{0,86},{1,87},{2,88},{3,89},{4,90},{5,91},{6,92},{7,93},{8,94},{9,... | collective-permute-start | bytes 98312 | tf_op jit(solution)/shard_map/ppermute | solution.py:349
  31.0 4.6 %all-to-all-done.arrived_ref = bf16[128,33,128]{2,1,0:T(8,128)(2,1)S(1)} async-done(((bf16[128,33,128]{2,1,0:T(8,128)(2,1)}), bf16[128,33,128]{2,1,0:T(8,128)(2,1)S(1)}, u32[]{:S(2)}, u32[]{:S(2)}) %all-to-all-start) | async-done | bytes 1081376 | tf_op jit(solution)/shard_map/all_to_all | solution.py:330
  35.7 0.0 copy-done.1
  35.7 1.7 %filter_spectrum.1 = (bf16[4096,256]{1,0:T(8,128)(2,1)S(1)}, f32[128,128]{1,0:T(8,128)S(1)}) custom-call(bf16[128,33,128]{2,1,0:T(8,128)(2,1)S(1)} %all-to-all-done.arrived_ref, f32[512,256]{1,0:T(8,128)S(1)} %copy-done.1), custom_call_target="tpu_custom_call" | custom-call | tf_op jit(solution)/shard_map/filter_spectrum/pallas_call | solution.py:275
  37.4 0.0 collective-permute-done.chunk1_ref
  37.4 0.0 collective-permute-done.1.chunk2_ref
  37.4 9.7 %convolution.1 = bf16[4096,128]{1,0:T(8,128)(2,1)S(1)} custom-call(s32[1]{0:T(128)} %bitcast.me_ref, bf16[4096,256]{1,0:T(8,128)(2,1)S(1)} %get-tuple-element.11.spectrum_ref, f32[128,128]{1,0:T(8,128)S(1)} %get-tuple-element.12.codes_s, bf16[32,512]{1,0:T(8,128)(2,1)S(1)} %get-tuple-element.13.chunk0_ref, ...), custom_call_target="tpu_custom_call" | custom-call | tf_op jit(solution)/shard_map/convolution/pallas_call | solution.py:287
  47.1 26.2 %all_to_all.10.received_ref = bf16[128,32,128]{2,1,0:T(8,128)(2,1)S(1)} all-to-all(bf16[128,32,128]{2,1,0:T(8,128)(2,1)S(1)} %bitcast.5), channel_id=1, replica_groups=mesh['row'=16,'col'=8] {'row','col'}, dimensions={0} | all-to-all | bytes 2097152 | tf_op jit(solution)/shard_map/all_to_all | solution.py:353
  73.3 1.3 %unpack.1 = bf16[128,4096]{1,0:T(8,128)(2,1)} custom-call(bf16[128,32,128]{2,1,0:T(8,128)(2,1)S(1)} %all_to_all.10.received_ref), custom_call_target="tpu_custom_call" | custom-call | tf_op jit(solution)/shard_map/unpack/pallas_call | solution.py:356
  (1 shorter events, 0.0 us)
Async XLA Ops:
  2.8 11.2 %copy-start.5 = (bf16[8192]{0:T(1024)(128)(2,1)S(1)}, bf16[8192]{0:T(1024)(128)(2,1)}, u32[]{:S(2)}) copy-start(bf16[8192]{0:T(1024)(128)(2,1)} %param.10) | copy-start | bytes 49156
  2.8 11.2 %copy-start.2 = (bf16[8192,96]{0,1:T(8,128)(2,1)S(1)}, bf16[8192,96]{0,1:T(8,128)(2,1)}, u32[]{:S(2)}) copy-start(bf16[8192,96]{0,1:T(8,128)(2,1)} %param.11) | copy-start | bytes 4718596
  2.8 11.2 %copy-start.4 = (f32[4096]{0:T(1024)S(1)}, f32[4096]{0:T(1024)}, u32[]{:S(2)}) copy-start(f32[4096]{0:T(1024)} %param.14) | copy-start | bytes 49156
  2.8 32.8 %all-to-all-start = ((bf16[128,33,128]{2,1,0:T(8,128)(2,1)}), bf16[128,33,128]{2,1,0:T(8,128)(2,1)S(1)}, u32[]{:S(2)}, u32[]{:S(2)}) async-start(bf16[128,33,128]{2,1,0:T(8,128)(2,1)} %pack.1), calls=%async_computation | async-start | bytes 2621440 | tf_op jit(solution)/shard_map/all_to_all | solution.py:330
  14.1 3.4 %copy-start = (bf16[512,8192]{1,0:T(8,128)(2,1)S(1)}, bf16[512,8192]{1,0:T(8,128)(2,1)}, u32[]{:S(2)}) copy-start(bf16[512,8192]{1,0:T(8,128)(2,1)} %embedding_ref.1) | copy-start | bytes 25165828
  17.5 1.0 %copy-start.3 = (f32[7,12288]{1,0:T(8,128)S(1)}, f32[7,12288]{1,0:T(8,128)}, u32[]{:S(2)}) copy-start(f32[7,12288]{1,0:T(8,128)} %taps_hbm.1) | copy-start | bytes 1032196
  18.5 17.2 %copy-start.1 = (f32[512,256]{1,0:T(8,128)S(1)}, f32[512,256]{1,0:T(8,128)}, u32[]{:S(2)}) copy-start(f32[512,256]{1,0:T(8,128)} %constant.28.clone.constants_ref) | copy-start | bytes 1572868
  24.6 12.8 %collective-permute-start = (bf16[32,512]{1,0:T(8,128)(2,1)}, bf16[32,512]{1,0:T(8,128)(2,1)S(1)}, u32[]{:S(2)}, u32[]{:S(2)}) collective-permute-start(bf16[32,512]{1,0:T(8,128)(2,1)} %get-tuple-element.14), channel_id=1, source_target_pairs={{0,43},{1,44},{2,45},{3,46},{4,47},{5,48},{6,49},{7,50},{8,51},{9,... | collective-permute-start | bytes 98312 | tf_op jit(solution)/shard_map/ppermute | solution.py:349
  29.1 8.3 %collective-permute-start.1 = (bf16[32,512]{1,0:T(8,128)(2,1)S(1)}, bf16[32,512]{1,0:T(8,128)(2,1)S(1)}, u32[]{:S(2)}, u32[]{:S(2)}) collective-permute-start(bf16[32,512]{1,0:T(8,128)(2,1)S(1)} %get-tuple-element.15), channel_id=1, source_target_pairs={{0,86},{1,87},{2,88},{3,89},{4,90},{5,91},{6,92},{7,93},{8,94},{9,... | collective-permute-start | bytes 98312 | tf_op jit(solution)/shard_map/ppermute | solution.py:349

commit v5 on v4

--- a/solution.py
+++ b/solution.py
@@ -105,13 +105,22 @@
             )
 
 
-def unpack_kernel(received_ref, out_ref):
+def unpack_kernel(received_ref, out_hbm, out_ref, sent):
     count, width, positions = received_ref.shape
     inverse = pow(3, -1, count)
     group = LANES // width
+    part = out_ref.shape[1] // 4
+    copies = []
     for q in range(0, count, group):
         rows = [received_ref[(q + e) * inverse % count].astype(F32) for e in range(group)]
         out_ref[:, q * width : (q + group) * width] = jnp.concatenate(rows, axis=0).T.astype(BF16)
+        end = (q + group) * width
+        if end % part == 0:
+            at = pl.ds(end - part, part)
+            copies.append(pltpu.make_async_copy(out_ref.at[:, at], out_hbm.at[:, at], sent.at[len(copies)]))
+            copies[-1].start()
+    for copy in copies:
+        copy.wait()
 
 
 def matrices(constants_ref):
@@ -186,52 +195,58 @@
     parts = [chunks[(me + g * blocks) % 3] for g in range(3)]
     folded = jnp.concatenate([x[:, :half] for x in parts] + [x[:, half:] for x in parts], axis=0)
 
-    def look_up(step, carry):
+    entry = (lax.broadcasted_iota(jnp.int32, (16, blocks), 0).astype(F32) + 1.0).astype(BF16)
+
+    def look_up(positions):
         found = []
         hots = []
-        entry = lax.broadcasted_iota(jnp.int32, (half, blocks), 0).astype(F32) + 1.0
-        for h in range(AT_ONCE):
-            code = codes_s[pl.ds(AT_ONCE * step + h, 1), :]
+        for p in positions:
+            code = codes_s[p : p + 1, :]
             found.append(code)
-            hots.append((entry == jnp.abs(code)).astype(F32).astype(BF16))
+            size = jnp.broadcast_to(jnp.abs(code), (16, blocks)).astype(BF16)
+            equal = [jnp.where(entry == size - BF16(r), BF16(1), BF16(0)).astype(BF16) for r in range(0, half, 16)]
+            hots.append(jnp.concatenate(equal, axis=0))
         both = dot(folded, jnp.concatenate(hots, axis=1))
-        for h in range(AT_ONCE):
+        for h, p in enumerate(positions):
             here = both[:, h * blocks : (h + 1) * blocks]
-            begin = pl.multiple_of((AT_ONCE * step + h + 8) * rows, 8)
-            mixed[pl.ds(begin, rows), :] = jnp.where(found[h] < 0.0, here[rows:], here[:rows])
-        return carry
-
-    lax.fori_loop(0, lanes // AT_ONCE, look_up, 0)
+            mixed[(p + 8) * rows : (p + 9) * rows, :] = jnp.where(found[h] < 0.0, here[rows:], here[:rows])
+
+    def short_filter(positions):
+        for c in range(0, width, 8):
+            taps = [
+                [jnp.broadcast_to(columns[c : c + 8, 8 * g + i : 8 * g + i + 1], (8, blocks)) for i in range(tap_count)]
+                for g in range(3)
+            ]
+
+            def at(p, g):
+                begin = (p + 8) * rows + g * width + c
+                return mixed[begin : begin + 8, :]
+
+            window = [[at(positions[0] - i, g) for i in range(1, tap_count)] for g in range(3)]
+            for p in positions:
+                total = []
+                for g in range(3):
+                    here = at(p, g)
+                    value = taps[g][0] * here
+                    for i in range(1, tap_count):
+                        value = value + taps[g][i] * window[g][i - 1]
+                    total.append(value)
+                    window[g] = [here] + window[g][:-1]
+                gate[p * pitch + c : p * pitch + c + 8, :] = total[0]
+                signal[p * pitch + c : p * pitch + c + 8, :] = total[1] * total[2]
+
+    steps = [range(p, p + AT_ONCE) for p in range(0, lanes, AT_ONCE)]
+    look_up(steps[-1])
     block = lax.broadcasted_iota(jnp.int32, (rows, blocks), 1)
     for i in range(1, tap_count):
         last = mixed[(lanes + 8 - i) * rows : (lanes + 9 - i) * rows, :]
         mixed[(8 - i) * rows : (9 - i) * rows, :] = jnp.where(block == 0, 0.0, pltpu.roll(last, 1, 1))
-
-    for c in range(0, width, 8):
-        taps = [
-            [jnp.broadcast_to(columns[c : c + 8, 8 * g + i : 8 * g + i + 1], (8, blocks)) for i in range(tap_count)]
-            for g in range(3)
-        ]
-
-        def at(p, g):
-            return mixed[pl.ds(pl.multiple_of((p + 8) * rows + g * width + c, 8), 8), :]
-
-        def filter_step(p, window):
-            later = []
-            total = []
-            for g in range(3):
-                here = at(p, g)
-                value = taps[g][0] * here
-                for i in range(1, tap_count):
-                    value = value + taps[g][i] * window[g][i - 1]
-                total.append(value)
-                later.append((here,) + window[g][:-1])
-            gate[pl.ds(p * pitch + c, 8), :] = total[0]
-            signal[pl.ds(p * pitch + c, 8), :] = total[1] * total[2]
-            return tuple(later)
-
-        before = tuple(tuple(at(-i, g) for i in range(1, tap_count)) for g in range(3))
-        lax.fori_loop(0, lanes, filter_step, before, unroll=8)
+    for k, step in enumerate(steps):
+        if k == 0:
+            look_up(step)
+        if k + 1 < len(steps) - 1:
+            look_up(steps[k + 1])
+        short_filter(step)
 
     cos, sin, first, second, second_back, first_back = matrices(constants_ref)
 
@@ -356,8 +371,9 @@
     return pl.pallas_call(
         unpack_kernel,
         in_specs=[vmem],
-        out_specs=vmem,
+        out_specs=hbm,
         out_shape=jax.ShapeDtypeStruct((positions, channels), BF16),
+        scratch_shapes=[pltpu.VMEM((positions, channels), BF16), pltpu.SemaphoreType.DMA((4,))],
         compiler_params=pltpu.CompilerParams(vmem_limit_bytes=16 * 1024 * 1024),
         name="unpack",
     )(received)

time: 74.9 us -> 72.9 us (0.973)
  Pallas kernels: 21.7 us -> 19.6 us
    pallas_call x1, Pallas kernels: 9.66 us -> 7.73 us  [conv_call(): pl.pallas_call(functools.partial(conv_kernel, tap_count=tap_count, pitch=...]
where the time goes in v5:
time: 72.9 us; the launch traced here: 72.7 us
  blocking collectives  26.2 us (36%)
  Pallas kernels  19.6 us (27%)
  starting transfers between devices  17.7 us (24%)
  waiting for transfers between devices  4.47 us (6%)
  local copies, waits for them, and re-layouts  4.41 us (6%)
    all_to_all x1, blocking collectives, local(): lax.all_to_all(out.reshape(devices, width, positions), AXES, split_axis=0...  26.2 us
    all_to_all x1, starting transfers between devices, local(): lax.all_to_all(sent, AXES, split_axis=0, concat_axis=0, tiled=True)  11.1 us
    pallas_call x1, Pallas kernels, conv_call(): pl.pallas_call(functools.partial(conv_kernel, tap_count=tap_count, pitch=...  7.73 us
    ppermute x2, starting transfers between devices, local(): lax.ppermute(own[j], AXES, [(d, (d + j * inverse) % devices) for d in ran...  6.58 us
    pallas_call x1, Pallas kernels, local(): pl.pallas_call(table_kernel, in_specs=[pl.BlockSpec(memory_space=pltpu.SM...  6.17 us
    all_to_all x1, waiting for transfers between devices, local(): lax.all_to_all(sent, AXES, split_axis=0, concat_axis=0, tiled=True)  4.46 us
    unnamed x12, local copies, waits for them, and re-layouts  4.39 us
    pallas_call x1, Pallas kernels, local(): pl.pallas_call(functools.partial(pack_kernel, half=half), in_specs=[hbm,...  2.8 us
  transfers between devices with their start and end apart: 3, of which 1 were waited for; matrix products, arithmetic and copies ran while one was open for 0% of the time, Pallas kernels for 11%

profile of v5, /device:TPU:0, one launch (start us, length us, event | category | flops | bytes accessed | tf_op | source)
XLA Modules:
  0.0 72.7 jit_solution(795209765910298236)
XLA Ops:
  0.0 2.8 %pack.1 = bf16[128,33,128]{2,1,0:T(8,128)(2,1)} custom-call(f32[128,4096]{1,0:T(8,128)} %filter_hbm.1, s32[1,128]{1,0:T(1,128)} %bitcast.8), custom_call_target="tpu_custom_call" | custom-call | tf_op jit(solution)/shard_map/pack/pallas_call | solution.py:332
  2.8 0.0 copy-start.5
  2.8 0.0 copy-start.2
  2.8 0.0 copy-start.4
  2.8 11.1 %all-to-all-start = ((bf16[128,33,128]{2,1,0:T(8,128)(2,1)}), bf16[128,33,128]{2,1,0:T(8,128)(2,1)S(1)}, u32[]{:S(2)}, u32[]{:S(2)}) async-start(bf16[128,33,128]{2,1,0:T(8,128)(2,1)} %pack.1), calls=%async_computation | async-start | bytes 2621440 | tf_op jit(solution)/shard_map/all_to_all | solution.py:345
  14.0 0.0 copy-done.5
  14.1 0.0 copy-done.2
  14.1 0.0 copy-done.4
  14.1 0.0 copy-start
  14.1 3.4 %copy-done = bf16[512,8192]{1,0:T(8,128)(2,1)S(1)} copy-done((bf16[512,8192]{1,0:T(8,128)(2,1)S(1)}, bf16[512,8192]{1,0:T(8,128)(2,1)}, u32[]{:S(2)}) %copy-start) | copy-done | bytes 8388632
  17.5 0.0 copy-start.3
  17.5 1.0 %copy-done.3 = f32[7,12288]{1,0:T(8,128)S(1)} copy-done((f32[7,12288]{1,0:T(8,128)S(1)}, f32[7,12288]{1,0:T(8,128)}, u32[]{:S(2)}) %copy-start.3) | copy-done | bytes 344088
  18.5 0.0 copy-start.1
  18.5 6.2 %table.1 = (bf16[32,512]{1,0:T(8,128)(2,1)S(1)}, bf16[32,512]{1,0:T(8,128)(2,1)}, bf16[32,512]{1,0:T(8,128)(2,1)S(1)}, f32[32,128]{1,0:T(8,128)S(1)}) custom-call(s32[1]{0:T(128)} %bitcast.me_ref, bf16[512,8192]{1,0:T(8,128)(2,1)S(1)} %copy-done, bf16[1,8192]{1,0:T(2,128)(2,1)S(1)} %broadcast_in_dim.11.gain_ref, bf16[96,8192]{1,0:T(8,128)(2,1)S(1)} %bitcast.6, ...), custom_call_target="tpu_custom_call" | custom-call | tf_op jit(solution)/shard_map/table/pallas_call | solution.py:348
  24.6 4.4 %collective-permute-start = (bf16[32,512]{1,0:T(8,128)(2,1)}, bf16[32,512]{1,0:T(8,128)(2,1)S(1)}, u32[]{:S(2)}, u32[]{:S(2)}) collective-permute-start(bf16[32,512]{1,0:T(8,128)(2,1)} %get-tuple-element.14), channel_id=1, source_target_pairs={{0,43},{1,44},{2,45},{3,46},{4,47},{5,48},{6,49},{7,50},{8,51},{9,... | collective-permute-start | bytes 98312 | tf_op jit(solution)/shard_map/ppermute | solution.py:364
  29.1 2.1 %collective-permute-start.1 = (bf16[32,512]{1,0:T(8,128)(2,1)S(1)}, bf16[32,512]{1,0:T(8,128)(2,1)S(1)}, u32[]{:S(2)}, u32[]{:S(2)}) collective-permute-start(bf16[32,512]{1,0:T(8,128)(2,1)S(1)} %get-tuple-element.15), channel_id=1, source_target_pairs={{0,86},{1,87},{2,88},{3,89},{4,90},{5,91},{6,92},{7,93},{8,94},{9,... | collective-permute-start | bytes 98312 | tf_op jit(solution)/shard_map/ppermute | solution.py:364
  31.2 4.5 %all-to-all-done.arrived_ref = bf16[128,33,128]{2,1,0:T(8,128)(2,1)S(1)} async-done(((bf16[128,33,128]{2,1,0:T(8,128)(2,1)}), bf16[128,33,128]{2,1,0:T(8,128)(2,1)S(1)}, u32[]{:S(2)}, u32[]{:S(2)}) %all-to-all-start) | async-done | bytes 1081376 | tf_op jit(solution)/shard_map/all_to_all | solution.py:345
  35.7 0.0 copy-done.1
  35.7 1.7 %filter_spectrum.1 = (bf16[4096,256]{1,0:T(8,128)(2,1)S(1)}, f32[128,128]{1,0:T(8,128)S(1)}) custom-call(bf16[128,33,128]{2,1,0:T(8,128)(2,1)S(1)} %all-to-all-done.arrived_ref, f32[512,256]{1,0:T(8,128)S(1)} %copy-done.1), custom_call_target="tpu_custom_call" | custom-call | tf_op jit(solution)/shard_map/filter_spectrum/pallas_call | solution.py:290
  37.4 0.0 collective-permute-done.chunk1_ref
  37.4 0.0 collective-permute-done.1.chunk2_ref
  37.4 7.7 %convolution.1 = bf16[4096,128]{1,0:T(8,128)(2,1)S(1)} custom-call(s32[1]{0:T(128)} %bitcast.me_ref, bf16[4096,256]{1,0:T(8,128)(2,1)S(1)} %get-tuple-element.11.spectrum_ref, f32[128,128]{1,0:T(8,128)S(1)} %get-tuple-element.12.codes_s, bf16[32,512]{1,0:T(8,128)(2,1)S(1)} %get-tuple-element.13.chunk0_ref, ...), custom_call_target="tpu_custom_call" | custom-call | tf_op jit(solution)/shard_map/convolution/pallas_call | solution.py:302
  45.2 26.2 %all_to_all.10.received_ref = bf16[128,32,128]{2,1,0:T(8,128)(2,1)S(1)} all-to-all(bf16[128,32,128]{2,1,0:T(8,128)(2,1)S(1)} %bitcast.5), channel_id=1, replica_groups=mesh['row'=16,'col'=8] {'row','col'}, dimensions={0} | all-to-all | bytes 2097152 | tf_op jit(solution)/shard_map/all_to_all | solution.py:368
  71.4 1.1 %unpack.1 = bf16[128,4096]{1,0:T(8,128)(2,1)} custom-call(bf16[128,32,128]{2,1,0:T(8,128)(2,1)S(1)} %all_to_all.10.received_ref), custom_call_target="tpu_custom_call" | custom-call | tf_op jit(solution)/shard_map/unpack/pallas_call | solution.py:371
  (1 shorter events, 0.0 us)
Async XLA Ops:
  2.8 11.2 %copy-start.5 = (bf16[8192]{0:T(1024)(128)(2,1)S(1)}, bf16[8192]{0:T(1024)(128)(2,1)}, u32[]{:S(2)}) copy-start(bf16[8192]{0:T(1024)(128)(2,1)} %param.10) | copy-start | bytes 49156
  2.8 11.2 %copy-start.2 = (bf16[8192,96]{0,1:T(8,128)(2,1)S(1)}, bf16[8192,96]{0,1:T(8,128)(2,1)}, u32[]{:S(2)}) copy-start(bf16[8192,96]{0,1:T(8,128)(2,1)} %param.11) | copy-start | bytes 4718596
  2.8 11.2 %copy-start.4 = (f32[4096]{0:T(1024)S(1)}, f32[4096]{0:T(1024)}, u32[]{:S(2)}) copy-start(f32[4096]{0:T(1024)} %param.14) | copy-start | bytes 49156
  2.8 32.8 %all-to-all-start = ((bf16[128,33,128]{2,1,0:T(8,128)(2,1)}), bf16[128,33,128]{2,1,0:T(8,128)(2,1)S(1)}, u32[]{:S(2)}, u32[]{:S(2)}) async-start(bf16[128,33,128]{2,1,0:T(8,128)(2,1)} %pack.1), calls=%async_computation | async-start | bytes 2621440 | tf_op jit(solution)/shard_map/all_to_all | solution.py:345
  14.1 3.4 %copy-start = (bf16[512,8192]{1,0:T(8,128)(2,1)S(1)}, bf16[512,8192]{1,0:T(8,128)(2,1)}, u32[]{:S(2)}) copy-start(bf16[512,8192]{1,0:T(8,128)(2,1)} %embedding_ref.1) | copy-start | bytes 25165828
  17.5 1.0 %copy-start.3 = (f32[7,12288]{1,0:T(8,128)S(1)}, f32[7,12288]{1,0:T(8,128)}, u32[]{:S(2)}) copy-start(f32[7,12288]{1,0:T(8,128)} %taps_hbm.1) | copy-start | bytes 1032196
  18.5 17.2 %copy-start.1 = (f32[512,256]{1,0:T(8,128)S(1)}, f32[512,256]{1,0:T(8,128)}, u32[]{:S(2)}) copy-start(f32[512,256]{1,0:T(8,128)} %constant.28.clone.constants_ref) | copy-start | bytes 1572868
  24.6 12.8 %collective-permute-start = (bf16[32,512]{1,0:T(8,128)(2,1)}, bf16[32,512]{1,0:T(8,128)(2,1)S(1)}, u32[]{:S(2)}, u32[]{:S(2)}) collective-permute-start(bf16[32,512]{1,0:T(8,128)(2,1)} %get-tuple-element.14), channel_id=1, source_target_pairs={{0,43},{1,44},{2,45},{3,46},{4,47},{5,48},{6,49},{7,50},{8,51},{9,... | collective-permute-start | bytes 98312 | tf_op jit(solution)/shard_map/ppermute | solution.py:364
  29.1 8.4 %collective-permute-start.1 = (bf16[32,512]{1,0:T(8,128)(2,1)S(1)}, bf16[32,512]{1,0:T(8,128)(2,1)S(1)}, u32[]{:S(2)}, u32[]{:S(2)}) collective-permute-start(bf16[32,512]{1,0:T(8,128)(2,1)S(1)} %get-tuple-element.15), channel_id=1, source_target_pairs={{0,86},{1,87},{2,88},{3,89},{4,90},{5,91},{6,92},{7,93},{8,94},{9,... | collective-permute-start | bytes 98312 | tf_op jit(solution)/shard_map/ppermute | solution.py:364

commit v6 on v5

--- a/solution.py
+++ b/solution.py
@@ -14,7 +14,7 @@
 AT_ONCE = 32
 PACK_VMEM = 62
 TABLE_VMEM = 20
-TOGETHER = 8
+TOGETHER = 16
 F32 = jnp.float32
 BF16 = jnp.bfloat16
 
@@ -100,7 +100,7 @@
             copies[1 + q * width // part].wait()
         turned = filter_ref[:, q * width : (q + group) * width].T.astype(BF16)
         for e in range(group):
-            out_ref[(q + e) * inverse % count] = jnp.concatenate(
+            out_ref[(q + e - 1) * inverse % count] = jnp.concatenate(
                 [turned[e * width : (e + 1) * width], code], axis=0
             )
 
@@ -112,7 +112,7 @@
     part = out_ref.shape[1] // 4
     copies = []
     for q in range(0, count, group):
-        rows = [received_ref[(q + e) * inverse % count].astype(F32) for e in range(group)]
+        rows = [received_ref[(q + e - 1) * inverse % count].astype(F32) for e in range(group)]
         out_ref[:, q * width : (q + group) * width] = jnp.concatenate(rows, axis=0).T.astype(BF16)
         end = (q + group) * width
         if end % part == 0:
@@ -344,7 +344,7 @@
     )(long_filter, token_ids[None])
     arrived = lax.all_to_all(sent, AXES, split_axis=0, concat_axis=0, tiled=True)
 
-    block = (3 * me % devices)[None].astype(jnp.int32)
+    block = ((3 * me + 1) % devices)[None].astype(jnp.int32)
     *own, columns = pl.pallas_call(
         table_kernel,
         in_specs=[pl.BlockSpec(memory_space=pltpu.SMEM), vmem, vmem, vmem, hbm, hbm],
@@ -360,9 +360,10 @@
         name="table",
     )(block, embedding, norm_gain[None], w_in.T, short_taps, skip_gain.reshape(channels // LANES, LANES))
     inverse = pow(3, -1, devices)
-    chunks = [own[0]] + [
-        lax.ppermute(own[j], AXES, [(d, (d + j * inverse) % devices) for d in range(devices)]) for j in (1, 2)
+    moved = [
+        lax.ppermute(own[1 + j], AXES, [(d, (d + j * inverse) % devices) for d in range(devices)]) for j in (-1, 1)
     ]
+    chunks = [moved[0], own[1], moved[1]]
 
     out = conv_call(block, arrived, *chunks, columns, constants, short_taps.shape[0])
     received = lax.all_to_all(

time: 72.9 us -> 72.2 us (level)
  waiting for transfers between devices: 4.47 us -> 6.21 us
  blocking collectives: 26.2 us -> 24.7 us
  starting transfers between devices: 17.7 us -> 16.6 us
    all_to_all x1, waiting for transfers between devices: 4.46 us -> 6.2 us  [local(): lax.all_to_all(sent, AXES, split_axis=0, concat_axis=0, tiled=True)]
    all_to_all x1, blocking collectives: 26.2 us -> 24.7 us  [local(): lax.all_to_all(out.reshape(devices, width, positions), AXES, split_axis=0...]
    ppermute x2, starting transfers between devices: 6.58 us -> 5.44 us  [local(): lax.ppermute(own[1 + j], AXES, [(d, (d + j * inverse) % devices) for d in...]
where the time goes in v6:
time: 72.2 us; the launch traced here: 72 us
  blocking collectives  24.7 us (34%)
  Pallas kernels  19.7 us (27%)
  starting transfers between devices  16.6 us (23%)
  waiting for transfers between devices  6.21 us (9%)
  local copies, waits for them, and re-layouts  4.41 us (6%)
    all_to_all x1, blocking collectives, local(): lax.all_to_all(out.reshape(devices, width, positions), AXES, split_axis=0...  24.7 us
    all_to_all x1, starting transfers between devices, local(): lax.all_to_all(sent, AXES, split_axis=0, concat_axis=0, tiled=True)  11.1 us
    pallas_call x1, Pallas kernels, conv_call(): pl.pallas_call(functools.partial(conv_kernel, tap_count=tap_count, pitch=...  7.89 us
    all_to_all x1, waiting for transfers between devices, local(): lax.all_to_all(sent, AXES, split_axis=0, concat_axis=0, tiled=True)  6.2 us
    pallas_call x1, Pallas kernels, local(): pl.pallas_call(table_kernel, in_specs=[pl.BlockSpec(memory_space=pltpu.SM...  6.16 us
    ppermute x2, starting transfers between devices, local(): lax.ppermute(own[1 + j], AXES, [(d, (d + j * inverse) % devices) for d in...  5.44 us
    unnamed x12, local copies, waits for them, and re-layouts  4.39 us
    pallas_call x1, Pallas kernels, local(): pl.pallas_call(functools.partial(pack_kernel, half=half), in_specs=[hbm,...  2.8 us
  transfers between devices with their start and end apart: 3, of which 1 were waited for; matrix products, arithmetic and copies ran while one was open for 0% of the time, Pallas kernels for 11%

profile of v6, /device:TPU:0, one launch (start us, length us, event | category | flops | bytes accessed | tf_op | source)
XLA Modules:
  0.0 72.0 jit_solution(6065856163915314291)
XLA Ops:
  0.0 2.8 %pack.1 = bf16[128,33,128]{2,1,0:T(8,128)(2,1)} custom-call(f32[128,4096]{1,0:T(8,128)} %filter_hbm.1, s32[1,128]{1,0:T(1,128)} %bitcast.8), custom_call_target="tpu_custom_call" | custom-call | tf_op jit(solution)/shard_map/pack/pallas_call | solution.py:332
  2.8 0.0 copy-start.5
  2.8 0.0 copy-start.2
  2.8 0.0 copy-start.4
  2.8 11.1 %all-to-all-start = ((bf16[128,33,128]{2,1,0:T(8,128)(2,1)}), bf16[128,33,128]{2,1,0:T(8,128)(2,1)S(1)}, u32[]{:S(2)}, u32[]{:S(2)}) async-start(bf16[128,33,128]{2,1,0:T(8,128)(2,1)} %pack.1), calls=%async_computation | async-start | bytes 2621440 | tf_op jit(solution)/shard_map/all_to_all | solution.py:345
  14.0 0.0 copy-done.5
  14.1 0.0 copy-done.2
  14.1 0.0 copy-done.4
  14.1 0.0 copy-start
  14.1 3.4 %copy-done = bf16[512,8192]{1,0:T(8,128)(2,1)S(1)} copy-done((bf16[512,8192]{1,0:T(8,128)(2,1)S(1)}, bf16[512,8192]{1,0:T(8,128)(2,1)}, u32[]{:S(2)}) %copy-start) | copy-done | bytes 8388632
  17.5 0.0 copy-start.3
  17.5 1.0 %copy-done.3 = f32[7,12288]{1,0:T(8,128)S(1)} copy-done((f32[7,12288]{1,0:T(8,128)S(1)}, f32[7,12288]{1,0:T(8,128)}, u32[]{:S(2)}) %copy-start.3) | copy-done | bytes 344088
  18.5 0.0 copy-start.1
  18.5 6.2 %table.1 = (bf16[32,512]{1,0:T(8,128)(2,1)}, bf16[32,512]{1,0:T(8,128)(2,1)S(1)}, bf16[32,512]{1,0:T(8,128)(2,1)S(1)}, f32[32,128]{1,0:T(8,128)S(1)}) custom-call(s32[1]{0:T(128)} %bitcast.me_ref, bf16[512,8192]{1,0:T(8,128)(2,1)S(1)} %copy-done, bf16[1,8192]{1,0:T(2,128)(2,1)S(1)} %broadcast_in_dim.11.gain_ref, bf16[96,8192]{1,0:T(8,128)(2,1)S(1)} %bitcast.6, ...), custom_call_target="tpu_custom_call" | custom-call | tf_op jit(solution)/shard_map/table/pallas_call | solution.py:348
  24.6 4.8 %collective-permute-start = (bf16[32,512]{1,0:T(8,128)(2,1)}, bf16[32,512]{1,0:T(8,128)(2,1)S(1)}, u32[]{:S(2)}, u32[]{:S(2)}) collective-permute-start(bf16[32,512]{1,0:T(8,128)(2,1)} %get-tuple-element.13), channel_id=1, source_target_pairs={{0,85},{1,86},{2,87},{3,88},{4,89},{5,90},{6,91},{7,92},{8,93},{9,... | collective-permute-start | bytes 98312 | tf_op jit(solution)/shard_map/ppermute | solution.py:364
  29.4 0.7 collective-permute-start.1
  30.1 6.2 %all-to-all-done.arrived_ref = bf16[128,33,128]{2,1,0:T(8,128)(2,1)S(1)} async-done(((bf16[128,33,128]{2,1,0:T(8,128)(2,1)}), bf16[128,33,128]{2,1,0:T(8,128)(2,1)S(1)}, u32[]{:S(2)}, u32[]{:S(2)}) %all-to-all-start) | async-done | bytes 1081376 | tf_op jit(solution)/shard_map/all_to_all | solution.py:345
  36.3 0.0 copy-done.1
  36.3 1.7 %filter_spectrum.1 = (bf16[4096,256]{1,0:T(8,128)(2,1)S(1)}, f32[128,128]{1,0:T(8,128)S(1)}) custom-call(bf16[128,33,128]{2,1,0:T(8,128)(2,1)S(1)} %all-to-all-done.arrived_ref, f32[512,256]{1,0:T(8,128)S(1)} %copy-done.1), custom_call_target="tpu_custom_call" | custom-call | tf_op jit(solution)/shard_map/filter_spectrum/pallas_call | solution.py:290
  38.0 0.0 collective-permute-done.chunk0_ref
  38.0 0.0 collective-permute-done.1.chunk2_ref
  38.0 7.9 %convolution.1 = bf16[4096,128]{1,0:T(8,128)(2,1)S(1)} custom-call(s32[1]{0:T(128)} %bitcast.me_ref, bf16[4096,256]{1,0:T(8,128)(2,1)S(1)} %get-tuple-element.11.spectrum_ref, f32[128,128]{1,0:T(8,128)S(1)} %get-tuple-element.12.codes_s, bf16[32,512]{1,0:T(8,128)(2,1)S(1)} %collective-permute-done.chunk0_ref, ...), custom_call_target="tpu_custom_call" | custom-call | tf_op jit(solution)/shard_map/convolution/pallas_call | solution.py:302
  45.9 24.7 %all_to_all.10.received_ref = bf16[128,32,128]{2,1,0:T(8,128)(2,1)S(1)} all-to-all(bf16[128,32,128]{2,1,0:T(8,128)(2,1)S(1)} %bitcast.5), channel_id=1, replica_groups=mesh['row'=16,'col'=8] {'row','col'}, dimensions={0} | all-to-all | bytes 2097152 | tf_op jit(solution)/shard_map/all_to_all | solution.py:369
  70.7 1.1 %unpack.1 = bf16[128,4096]{1,0:T(8,128)(2,1)} custom-call(bf16[128,32,128]{2,1,0:T(8,128)(2,1)S(1)} %all_to_all.10.received_ref), custom_call_target="tpu_custom_call" | custom-call | tf_op jit(solution)/shard_map/unpack/pallas_call | solution.py:372
  (1 shorter events, 0.0 us)
Async XLA Ops:
  2.8 11.2 %copy-start.5 = (bf16[8192]{0:T(1024)(128)(2,1)S(1)}, bf16[8192]{0:T(1024)(128)(2,1)}, u32[]{:S(2)}) copy-start(bf16[8192]{0:T(1024)(128)(2,1)} %param.10) | copy-start | bytes 49156
  2.8 11.2 %copy-start.2 = (bf16[8192,96]{0,1:T(8,128)(2,1)S(1)}, bf16[8192,96]{0,1:T(8,128)(2,1)}, u32[]{:S(2)}) copy-start(bf16[8192,96]{0,1:T(8,128)(2,1)} %param.11) | copy-start | bytes 4718596
  2.8 11.2 %copy-start.4 = (f32[4096]{0:T(1024)S(1)}, f32[4096]{0:T(1024)}, u32[]{:S(2)}) copy-start(f32[4096]{0:T(1024)} %param.14) | copy-start | bytes 49156
  2.8 33.4 %all-to-all-start = ((bf16[128,33,128]{2,1,0:T(8,128)(2,1)}), bf16[128,33,128]{2,1,0:T(8,128)(2,1)S(1)}, u32[]{:S(2)}, u32[]{:S(2)}) async-start(bf16[128,33,128]{2,1,0:T(8,128)(2,1)} %pack.1), calls=%async_computation | async-start | bytes 2621440 | tf_op jit(solution)/shard_map/all_to_all | solution.py:345
  14.1 3.4 %copy-start = (bf16[512,8192]{1,0:T(8,128)(2,1)S(1)}, bf16[512,8192]{1,0:T(8,128)(2,1)}, u32[]{:S(2)}) copy-start(bf16[512,8192]{1,0:T(8,128)(2,1)} %embedding_ref.1) | copy-start | bytes 25165828
  17.5 1.0 %copy-start.3 = (f32[7,12288]{1,0:T(8,128)S(1)}, f32[7,12288]{1,0:T(8,128)}, u32[]{:S(2)}) copy-start(f32[7,12288]{1,0:T(8,128)} %taps_hbm.1) | copy-start | bytes 1032196
  18.5 17.8 %copy-start.1 = (f32[512,256]{1,0:T(8,128)S(1)}, f32[512,256]{1,0:T(8,128)}, u32[]{:S(2)}) copy-start(f32[512,256]{1,0:T(8,128)} %constant.30.clone.constants_ref) | copy-start | bytes 1572868
  24.6 13.4 %collective-permute-start = (bf16[32,512]{1,0:T(8,128)(2,1)}, bf16[32,512]{1,0:T(8,128)(2,1)S(1)}, u32[]{:S(2)}, u32[]{:S(2)}) collective-permute-start(bf16[32,512]{1,0:T(8,128)(2,1)} %get-tuple-element.13), channel_id=1, source_target_pairs={{0,85},{1,86},{2,87},{3,88},{4,89},{5,90},{6,91},{7,92},{8,93},{9,... | collective-permute-start | bytes 98312 | tf_op jit(solution)/shard_map/ppermute | solution.py:364
  29.4 8.6 %collective-permute-start.1 = (bf16[32,512]{1,0:T(8,128)(2,1)S(1)}, bf16[32,512]{1,0:T(8,128)(2,1)S(1)}, u32[]{:S(2)}, u32[]{:S(2)}) collective-permute-start(bf16[32,512]{1,0:T(8,128)(2,1)S(1)} %get-tuple-element.15), channel_id=1, source_target_pairs={{0,43},{1,44},{2,45},{3,46},{4,47},{5,48},{6,49},{7,50},{8,51},{9,... | collective-permute-start | bytes 98312 | tf_op jit(solution)/shard_map/ppermute | solution.py:364

commit v7 on v6

--- a/solution.py
+++ b/solution.py
@@ -13,6 +13,7 @@
 LANES = 128
 AT_ONCE = 32
 PACK_VMEM = 62
+PIECES = 2
 TABLE_VMEM = 20
 TOGETHER = 16
 F32 = jnp.float32
@@ -84,9 +85,9 @@
     count, rows, positions = out_ref.shape
     width = rows - 1
     group = LANES // width
-    part = filter_hbm.shape[1] // 4
-    copies = [pltpu.make_async_copy(ids_hbm, ids_ref, arrived.at[4])]
-    for k in range(4):
+    part = filter_hbm.shape[1] // PIECES
+    copies = [pltpu.make_async_copy(ids_hbm, ids_ref, arrived.at[PIECES])]
+    for k in range(PIECES):
         at = pl.ds(k * part, part)
         copies.append(pltpu.make_async_copy(filter_hbm.at[:, at], filter_ref.at[:, at], arrived.at[k]))
     for copy in copies:
@@ -337,7 +338,7 @@
         scratch_shapes=[
             pltpu.VMEM((positions, channels), F32),
             pltpu.VMEM((1, positions), jnp.int32),
-            pltpu.SemaphoreType.DMA((5,)),
+            pltpu.SemaphoreType.DMA((PIECES + 1,)),
         ],
         compiler_params=pltpu.CompilerParams(vmem_limit_bytes=PACK_VMEM * 1024 * 1024),
         name="pack",

time: 72.2 us -> 72.3 us (level)
  no operation moved by 1% of the time
where the time goes in v7:
time: 72.3 us; the launch traced here: 72 us
  blocking collectives  24.7 us (34%)
  Pallas kernels  19.8 us (27%)
  starting transfers between devices  16.6 us (23%)
  waiting for transfers between devices  6.21 us (9%)
  local copies, waits for them, and re-layouts  4.41 us (6%)
    all_to_all x1, blocking collectives, local(): lax.all_to_all(out.reshape(devices, width, positions), AXES, split_axis=0...  24.7 us
    all_to_all x1, starting transfers between devices, local(): lax.all_to_all(sent, AXES, split_axis=0, concat_axis=0, tiled=True)  11.1 us
    pallas_call x1, Pallas kernels, conv_call(): pl.pallas_call(functools.partial(conv_kernel, tap_count=tap_count, pitch=...  7.89 us
    all_to_all x1, waiting for transfers between devices, local(): lax.all_to_all(sent, AXES, split_axis=0, concat_axis=0, tiled=True)  6.2 us
    pallas_call x1, Pallas kernels, local(): pl.pallas_call(table_kernel, in_specs=[pl.BlockSpec(memory_space=pltpu.SM...  6.16 us
    ppermute x2, starting transfers between devices, local(): lax.ppermute(own[1 + j], AXES, [(d, (d + j * inverse) % devices) for d in...  5.44 us
    unnamed x12, local copies, waits for them, and re-layouts  4.39 us
    pallas_call x1, Pallas kernels, local(): pl.pallas_call(functools.partial(pack_kernel, half=half), in_specs=[hbm,...  2.88 us
  transfers between devices with their start and end apart: 3, of which 1 were waited for; matrix products, arithmetic and copies ran while one was open for 0% of the time, Pallas kernels for 11%

profile of v7, /device:TPU:0, one launch (start us, length us, event | category | flops | bytes accessed | tf_op | source)
XLA Modules:
  0.0 72.0 jit_solution(6364413155748338950)
XLA Ops:
  0.0 2.9 %pack.1 = bf16[128,33,128]{2,1,0:T(8,128)(2,1)} custom-call(f32[128,4096]{1,0:T(8,128)} %filter_hbm.1, s32[1,128]{1,0:T(1,128)} %bitcast.8), custom_call_target="tpu_custom_call" | custom-call | tf_op jit(solution)/shard_map/pack/pallas_call | solution.py:333
  2.9 0.0 copy-start.5
  2.9 0.0 copy-start.2
  2.9 0.0 copy-start.4
  2.9 11.1 %all-to-all-start = ((bf16[128,33,128]{2,1,0:T(8,128)(2,1)}), bf16[128,33,128]{2,1,0:T(8,128)(2,1)S(1)}, u32[]{:S(2)}, u32[]{:S(2)}) async-start(bf16[128,33,128]{2,1,0:T(8,128)(2,1)} %pack.1), calls=%async_computation | async-start | bytes 2621440 | tf_op jit(solution)/shard_map/all_to_all | solution.py:346
  14.1 0.0 copy-done.5
  14.1 0.0 copy-done.2
  14.1 0.0 copy-done.4
  14.2 0.0 copy-start
  14.2 3.4 %copy-done = bf16[512,8192]{1,0:T(8,128)(2,1)S(1)} copy-done((bf16[512,8192]{1,0:T(8,128)(2,1)S(1)}, bf16[512,8192]{1,0:T(8,128)(2,1)}, u32[]{:S(2)}) %copy-start) | copy-done | bytes 8388632
  17.5 0.0 copy-start.3
  17.5 1.0 %copy-done.3 = f32[7,12288]{1,0:T(8,128)S(1)} copy-done((f32[7,12288]{1,0:T(8,128)S(1)}, f32[7,12288]{1,0:T(8,128)}, u32[]{:S(2)}) %copy-start.3) | copy-done | bytes 344088
  18.5 0.0 copy-start.1
  18.5 6.2 %table.1 = (bf16[32,512]{1,0:T(8,128)(2,1)}, bf16[32,512]{1,0:T(8,128)(2,1)S(1)}, bf16[32,512]{1,0:T(8,128)(2,1)S(1)}, f32[32,128]{1,0:T(8,128)S(1)}) custom-call(s32[1]{0:T(128)} %bitcast.me_ref, bf16[512,8192]{1,0:T(8,128)(2,1)S(1)} %copy-done, bf16[1,8192]{1,0:T(2,128)(2,1)S(1)} %broadcast_in_dim.11.gain_ref, bf16[96,8192]{1,0:T(8,128)(2,1)S(1)} %bitcast.6, ...), custom_call_target="tpu_custom_call" | custom-call | tf_op jit(solution)/shard_map/table/pallas_call | solution.py:349
  24.7 4.8 %collective-permute-start = (bf16[32,512]{1,0:T(8,128)(2,1)}, bf16[32,512]{1,0:T(8,128)(2,1)S(1)}, u32[]{:S(2)}, u32[]{:S(2)}) collective-permute-start(bf16[32,512]{1,0:T(8,128)(2,1)} %get-tuple-element.13), channel_id=1, source_target_pairs={{0,85},{1,86},{2,87},{3,88},{4,89},{5,90},{6,91},{7,92},{8,93},{9,... | collective-permute-start | bytes 98312 | tf_op jit(solution)/shard_map/ppermute | solution.py:365
  29.5 0.7 collective-permute-start.1
  30.1 6.2 %all-to-all-done.arrived_ref = bf16[128,33,128]{2,1,0:T(8,128)(2,1)S(1)} async-done(((bf16[128,33,128]{2,1,0:T(8,128)(2,1)}), bf16[128,33,128]{2,1,0:T(8,128)(2,1)S(1)}, u32[]{:S(2)}, u32[]{:S(2)}) %all-to-all-start) | async-done | bytes 1081376 | tf_op jit(solution)/shard_map/all_to_all | solution.py:346
  36.4 0.0 copy-done.1
  36.4 1.7 %filter_spectrum.1 = (bf16[4096,256]{1,0:T(8,128)(2,1)S(1)}, f32[128,128]{1,0:T(8,128)S(1)}) custom-call(bf16[128,33,128]{2,1,0:T(8,128)(2,1)S(1)} %all-to-all-done.arrived_ref, f32[512,256]{1,0:T(8,128)S(1)} %copy-done.1), custom_call_target="tpu_custom_call" | custom-call | tf_op jit(solution)/shard_map/filter_spectrum/pallas_call | solution.py:291
  38.1 0.0 collective-permute-done.chunk0_ref
  38.1 0.0 collective-permute-done.1.chunk2_ref
  38.1 7.9 %convolution.1 = bf16[4096,128]{1,0:T(8,128)(2,1)S(1)} custom-call(s32[1]{0:T(128)} %bitcast.me_ref, bf16[4096,256]{1,0:T(8,128)(2,1)S(1)} %get-tuple-element.11.spectrum_ref, f32[128,128]{1,0:T(8,128)S(1)} %get-tuple-element.12.codes_s, bf16[32,512]{1,0:T(8,128)(2,1)S(1)} %collective-permute-done.chunk0_ref, ...), custom_call_target="tpu_custom_call" | custom-call | tf_op jit(solution)/shard_map/convolution/pallas_call | solution.py:303
  46.0 24.7 %all_to_all.10.received_ref = bf16[128,32,128]{2,1,0:T(8,128)(2,1)S(1)} all-to-all(bf16[128,32,128]{2,1,0:T(8,128)(2,1)S(1)} %bitcast.5), channel_id=1, replica_groups=mesh['row'=16,'col'=8] {'row','col'}, dimensions={0} | all-to-all | bytes 2097152 | tf_op jit(solution)/shard_map/all_to_all | solution.py:370
  70.7 1.1 %unpack.1 = bf16[128,4096]{1,0:T(8,128)(2,1)} custom-call(bf16[128,32,128]{2,1,0:T(8,128)(2,1)S(1)} %all_to_all.10.received_ref), custom_call_target="tpu_custom_call" | custom-call | tf_op jit(solution)/shard_map/unpack/pallas_call | solution.py:373
  (1 shorter events, 0.0 us)
Async XLA Ops:
  2.9 11.2 %copy-start.5 = (bf16[8192]{0:T(1024)(128)(2,1)S(1)}, bf16[8192]{0:T(1024)(128)(2,1)}, u32[]{:S(2)}) copy-start(bf16[8192]{0:T(1024)(128)(2,1)} %param.10) | copy-start | bytes 49156
  2.9 11.2 %copy-start.2 = (bf16[8192,96]{0,1:T(8,128)(2,1)S(1)}, bf16[8192,96]{0,1:T(8,128)(2,1)}, u32[]{:S(2)}) copy-start(bf16[8192,96]{0,1:T(8,128)(2,1)} %param.11) | copy-start | bytes 4718596
  2.9 11.2 %copy-start.4 = (f32[4096]{0:T(1024)S(1)}, f32[4096]{0:T(1024)}, u32[]{:S(2)}) copy-start(f32[4096]{0:T(1024)} %param.14) | copy-start | bytes 49156
  2.9 33.4 %all-to-all-start = ((bf16[128,33,128]{2,1,0:T(8,128)(2,1)}), bf16[128,33,128]{2,1,0:T(8,128)(2,1)S(1)}, u32[]{:S(2)}, u32[]{:S(2)}) async-start(bf16[128,33,128]{2,1,0:T(8,128)(2,1)} %pack.1), calls=%async_computation | async-start | bytes 2621440 | tf_op jit(solution)/shard_map/all_to_all | solution.py:346
  14.2 3.4 %copy-start = (bf16[512,8192]{1,0:T(8,128)(2,1)S(1)}, bf16[512,8192]{1,0:T(8,128)(2,1)}, u32[]{:S(2)}) copy-start(bf16[512,8192]{1,0:T(8,128)(2,1)} %embedding_ref.1) | copy-start | bytes 25165828
  17.5 1.0 %copy-start.3 = (f32[7,12288]{1,0:T(8,128)S(1)}, f32[7,12288]{1,0:T(8,128)}, u32[]{:S(2)}) copy-start(f32[7,12288]{1,0:T(8,128)} %taps_hbm.1) | copy-start | bytes 1032196
  18.5 17.8 %copy-start.1 = (f32[512,256]{1,0:T(8,128)S(1)}, f32[512,256]{1,0:T(8,128)}, u32[]{:S(2)}) copy-start(f32[512,256]{1,0:T(8,128)} %constant.30.clone.constants_ref) | copy-start | bytes 1572868
  24.7 13.4 %collective-permute-start = (bf16[32,512]{1,0:T(8,128)(2,1)}, bf16[32,512]{1,0:T(8,128)(2,1)S(1)}, u32[]{:S(2)}, u32[]{:S(2)}) collective-permute-start(bf16[32,512]{1,0:T(8,128)(2,1)} %get-tuple-element.13), channel_id=1, source_target_pairs={{0,85},{1,86},{2,87},{3,88},{4,89},{5,90},{6,91},{7,92},{8,93},{9,... | collective-permute-start | bytes 98312 | tf_op jit(solution)/shard_map/ppermute | solution.py:365
  29.5 8.6 %collective-permute-start.1 = (bf16[32,512]{1,0:T(8,128)(2,1)S(1)}, bf16[32,512]{1,0:T(8,128)(2,1)S(1)}, u32[]{:S(2)}, u32[]{:S(2)}) collective-permute-start(bf16[32,512]{1,0:T(8,128)(2,1)S(1)} %get-tuple-element.15), channel_id=1, source_target_pairs={{0,43},{1,44},{2,45},{3,46},{4,47},{5,48},{6,49},{7,50},{8,51},{9,... | collective-permute-start | bytes 98312 | tf_op jit(solution)/shard_map/ppermute | solution.py:365
